TPU v7x, 32 devices: a whole 2x2x4 slice. The times are simulated.
32 devices in a mesh: group: 2 (over y), slab: 4 (over z), plane: 4 (over x, core).
Axes of the slice: x: 2, y: 2, z: 4, core: 2. Of those that a mesh axis runs over, the one named last changes fastest.
Arguments:
- fields: float32 [2, 32, 128, 1024], P('group', None, 'slab', 'plane'), may hold values from 0 to 2
- evap_rates: float32 [32], replicated, may hold values from 0.05 to 0.5
- coal_kernel: bfloat16 [32, 1024], replicated, may hold values from -0.1875 to 0.1875
- plume_width: float32 [8], replicated, may hold values from 1 to 8
- owner_map: int32 [16, 2048], P(('slab', 'plane')), may hold values from 0 to 15, as said below
- deposit_cell: int32 [16, 2048], P(('slab', 'plane')), may hold values from 0 to 8191
- plume_ids: int32 [16, 2048], P(('slab', 'plane')), may hold values from 0 to 7
Outputs:
- new_fields: float32 [2, 32, 128, 1024], P('group', None, 'slab', 'plane')
Inputs may be any that keep to these rules, and one draw needn't show every extreme that they name: `owner_map`: among the 2048 rows of one index of the first dimension, at most 256 name any one spray block, and one block is named by exactly 256 of them at every index.
All inputs are finite; a program needn't handle non-finite values.
Results may differ from a plain program's by a relative error of at most 0.0014.
Values may be sent and summed in bfloat16 or wider, within the bound.
A program may use at most 64 MiB of HBM per device.

v0:
```python
import functools

import jax
import jax.numpy as jnp
import numpy as np
from jax import lax
from jax.experimental import pallas as pl
from jax.experimental.pallas import tpu as pltpu
from jax.sharding import PartitionSpec as P

MESH = pl.DeviceIdType.MESH
F32 = jnp.float32
BF16 = jnp.bfloat16
LANES = 128
SLOTS = 256
CHUNK = 4
SOURCES = 4
VMEM_BYTES = 63 * 1024 * 1024

cfl_nozzle = 0.35
diffusion = 0.2
relax_rate = 5.0
relax_step = 0.1
collide_step = 0.25


def fold_matrix(sections):
    kept = [(i, j) for i in range(sections) for j in range(i // 8 * 8, sections)]
    fold = np.zeros((sections * sections, len(kept)), np.float32)
    for q, (i, j) in enumerate(kept):
        fold[i * sections + j, q] = 1.0
        if j // 8 > i // 8:
            fold[j * sections + i, q] = 1.0
    return fold


def pair_terms(m):
    sections, width = m.shape
    pieces = []
    for i in range(sections):
        low = i // 8 * 8
        pieces.append(jnp.broadcast_to(m[i : i + 1], (sections - low, width)) * m[low:])
    return jnp.concatenate(pieces, axis=0).astype(BF16)


def split_hi_lo(x):
    hi = x.astype(BF16)
    lo = (x - hi.astype(F32)).astype(BF16)
    return hi, lo


def dot_last(a, b):
    return lax.dot_general(a, b, (((1,), (1,)), ((), ())), preferred_element_type=F32)


def kernel(
    n_slab, n_plane, sections, ca, cb, exit_rows,
    fields_hbm, evap_hbm, coal_hbm, fold_hbm, width_hbm, owner_hbm, cell_hbm, pid_hbm,
    out_hbm,
    fbuf, tbuf, hbuf, obuf, fold, cols_out, cols_in, par, send_buf, recv_buf,
    evap_ref, coal_ref, width_ref, owner_ref, cell_ref, pid_ref, picks, in_slot,
    in_sem, out_sem, arg_sem, halo_send, halo_recv, row_send, row_recv,
):
    owners = n_slab * n_plane
    plumes = width_ref.shape[0]
    rows = sections * ca
    g = lax.axis_index("group")
    s = lax.axis_index("slab")
    p = lax.axis_index("plane")
    me = s * n_plane + p

    load = pltpu.make_async_copy(fields_hbm, fbuf, in_sem)
    load.start()
    nozzle_args = [
        pltpu.make_async_copy(source, target, arg_sem.at[k])
        for k, (source, target) in enumerate(
            ((owner_hbm, owner_ref), (cell_hbm, cell_ref), (pid_hbm, pid_ref))
        )
    ]
    spray_args = [
        pltpu.make_async_copy(source, target, arg_sem.at[k])
        for k, (source, target) in enumerate(
            ((evap_hbm, evap_ref), (width_hbm, width_ref), (coal_hbm, coal_ref), (fold_hbm, fold))
        )
    ]

    @pl.when(g == 0)
    def _():
        for copy in nozzle_args:
            copy.start()

    @pl.when(g == 1)
    def _():
        for copy in spray_args:
            copy.start()

    barrier = pltpu.get_barrier_semaphore()
    sides = [
        (s > 0, (g, s - 1, p)),
        (s < n_slab - 1, (g, s + 1, p)),
        (p > 0, (g, s, p - 1)),
        (p < n_plane - 1, (g, s, p + 1)),
    ]
    near = 0
    for there, target in sides:
        near = near + there.astype(jnp.int32)

        @pl.when(there)
        def _():
            pl.semaphore_signal(barrier, inc=1, device_id=target, device_id_type=MESH)

    @pl.when(g == 1)
    def _():
        @pl.loop(0, owners)
        def _(o):
            pl.semaphore_signal(
                barrier, inc=1, device_id=(0, o // n_plane, o % n_plane), device_id_type=MESH
            )

    load.wait()

    def lines(a, h):
        return pl.ds(a // 8 * 16 + h * 8 + a % 8, sections, stride=2 * ca)

    def gather_row(ref, a):
        return jnp.concatenate([ref[lines(a, h), :] for h in range(2)], axis=1)

    def half(ref, h):
        return ref[...].reshape(rows // 8, 2, 8, LANES)[:, h].reshape(rows, LANES)

    for a in (0, ca - 1):
        tbuf[a + 1] = gather_row(fbuf, a)

    def halo(kind, target):
        source, landing = (
            (tbuf.at[ca], tbuf.at[0]),
            (tbuf.at[1], tbuf.at[ca + 1]),
            (cols_out.at[1], cols_in.at[0]),
            (cols_out.at[0], cols_in.at[1]),
        )[kind]
        return pltpu.make_async_remote_copy(
            src_ref=source,
            dst_ref=landing,
            send_sem=halo_send.at[kind],
            recv_sem=halo_recv.at[kind],
            device_id=target,
            device_id_type=MESH,
        )

    pl.semaphore_wait(barrier, near + jnp.where(g == 0, owners, 0))

    outgoing = (sides[1], sides[0], sides[3], sides[2])
    def start_halo(kinds):
        for kind in kinds:

            @pl.when(outgoing[kind][0])
            def _():
                halo(kind, outgoing[kind][1]).start()

    start_halo((0, 1))

    lane = lax.broadcasted_iota(jnp.int32, (8, LANES), 1)
    for h, at in ((0, 0), (1, LANES - 1)):
        select = (lane == at).astype(BF16)
        cols_out[h] = dot_last(select, half(fbuf, h).astype(BF16))[0:1]

    start_halo((2, 3))

    @pl.loop(1, ca - 1)
    def _(a):
        tbuf[a + 1] = gather_row(fbuf, a)

    for kind, landing in enumerate((tbuf.at[0], tbuf.at[ca + 1], cols_in.at[0], cols_in.at[1])):

        @pl.when(jnp.logical_not(sides[kind][0]))
        def _():
            landing[...] = jnp.zeros(landing.shape, F32)

    def finish_halo():
        for kind in range(4):

            @pl.when(outgoing[kind][0])
            def _():
                halo(kind, outgoing[kind][1]).wait_send()

            @pl.when(sides[kind][0])
            def _():
                halo(kind, outgoing[kind][1]).wait_recv()

        sub = lax.broadcasted_iota(jnp.int32, (16, cb), 0)
        lanes = lax.broadcasted_iota(jnp.int32, (16, cb), 1)
        stack = jnp.concatenate([cols_in[0], cols_in[1], jnp.zeros((14, rows), F32)], axis=0)
        place = jnp.logical_or(
            jnp.logical_and(sub == 0, lanes == 0), jnp.logical_and(sub == 1, lanes == cb - 1)
        ).astype(BF16)
        placed = jnp.dot(stack.T.astype(BF16), place, preferred_element_type=F32)
        for h in range(2):
            hbuf[h] = placed[:, h * LANES : (h + 1) * LANES]

    col_lane = lax.broadcasted_iota(jnp.int32, (sections, cb), 1)
    col_row = lax.broadcasted_iota(jnp.int32, (sections, cb), 0)

    def column_halo(a):
        return jnp.concatenate(
            [hbuf[h, pl.ds(a, sections, stride=ca), :] for h in range(2)], axis=1
        )

    def neighbours(a):
        c = tbuf[a + 1]
        up = tbuf[a]
        left = jnp.where(col_lane == 0, 0.0, pltpu.roll(c, 1, 1))
        right = jnp.where(col_lane == cb - 1, 0.0, pltpu.roll(c, cb - 1, 1))
        lap = up + tbuf[a + 2] + (left + right + column_halo(a)) - 4.0 * c
        return c, up, lap

    def scatter_row(a, value):
        for h in range(2):
            obuf[lines(a, h), :] = value[:, h * LANES : (h + 1) * LANES]

    store = pltpu.make_async_copy(obuf, out_hbm, out_sem)

    @pl.when(g == 0)
    def _():
        for copy in nozzle_args:
            copy.wait()
        owner = owner_ref[...]
        slots = []
        below = lax.broadcasted_iota(jnp.int32, (256, 256), 0)
        after = lax.broadcasted_iota(jnp.int32, (256, 256), 1)
        upto = (below <= after).astype(BF16)
        names = lax.broadcasted_iota(jnp.int32, (owners, 256), 0)
        carry = jnp.zeros((owners, 1), F32)
        for j in range(exit_rows // 256):
            hit = (owner[:, j * 256 : (j + 1) * 256] == names).astype(F32)
            count = jnp.dot(hit.astype(BF16), upto, preferred_element_type=F32) + carry
            slots.append(jnp.sum(hit * (count - 1.0), axis=0, keepdims=True))
            carry = count[:, 255:256]
        slot = jnp.concatenate(slots, axis=1)
        cell = cell_ref[...]
        across = jnp.bitwise_and(cell, cb - 1)
        along = jnp.right_shift(cell, cb.bit_length() - 1)
        par[4:5] = pid_ref[...].astype(F32)
        par[5:6] = along.astype(F32)
        par[6:7] = across.astype(F32)
        par[7:8] = jnp.zeros((1, exit_rows), F32)
        places = lax.broadcasted_iota(jnp.int32, (SLOTS, exit_rows), 0).astype(F32)
        in_slot[...] = (slot == places).astype(BF16)
        group = 16
        label = jnp.right_shift(lax.broadcasted_iota(jnp.int32, (group * 8, exit_rows), 0), 3)

        @pl.loop(0, owners // group)
        def _(b):
            picks[pl.ds(pl.multiple_of(b * group * 8, group * 8), group * 8)] = (
                owner == label + b * group
            ).astype(BF16)

        halve = jnp.where(
            jnp.right_shift(lax.broadcasted_iota(jnp.int32, (cb, cb // 2), 0), 1)
            == lax.broadcasted_iota(jnp.int32, (cb, cb // 2), 1),
            0.25,
            0.0,
        ).astype(BF16)

        finish_halo()

        layers = sections // 4
        plane_row = lax.broadcasted_iota(jnp.int32, (ca, cb), 0)
        plane_lane = lax.broadcasted_iota(jnp.int32, (ca, cb), 1)

        def plane(k):
            tiles = fbuf[pl.ds(k * 2 * ca, 2 * ca), :].reshape(ca // 8, 2, 8, LANES)
            return jnp.concatenate([tiles[:, h].reshape(ca, LANES) for h in range(2)], axis=1)

        def plane_lap(c, k):
            up = jnp.where(plane_row == 0, tbuf[0, k : k + 1], pltpu.roll(c, 1, 0))
            down = jnp.where(
                plane_row == ca - 1, tbuf[ca + 1, k : k + 1], pltpu.roll(c, ca - 1, 0)
            )
            left = jnp.where(plane_lane == 0, 0.0, pltpu.roll(c, 1, 1))
            right = jnp.where(plane_lane == cb - 1, 0.0, pltpu.roll(c, cb - 1, 1))
            at = pl.ds(k * ca, ca)
            halo_col = jnp.concatenate([hbuf[h, at] for h in range(2)], axis=1)
            return up + down + (left + right + halo_col) - 4.0 * c

        last = [v * layers + layers - 1 for v in range(4)]
        d, m, q, e = (plane(k) for k in last)
        if layers > 1:
            dm, dq, de = (x - plane(k - 1) for x, k in zip((m, q, e), last[1:]))
        else:
            dm, dq, de = m, q, e
        relaxing = relax_rate / (1.0 + d * d)
        exits = [
            m - cfl_nozzle * (dm + dq) + diffusion * plane_lap(m, last[1]),
            q
            + relax_step * relaxing * (e - q)
            - cfl_nozzle * dq
            + diffusion * plane_lap(q, last[2]),
            e - cfl_nozzle * de + diffusion * plane_lap(e, last[3]),
        ]
        paired = jnp.concatenate([x + pltpu.roll(x, ca - 1, 0) for x in exits], axis=0)
        hi = paired.astype(BF16)
        rest = paired - hi.astype(F32)
        mid, low = split_hi_lo(rest)
        sums = jnp.dot(
            jnp.concatenate([hi, mid, low], axis=0), halve, preferred_element_type=F32
        )
        coarse = sums[: 3 * ca] + sums[3 * ca : 6 * ca] + sums[6 * ca :]
        flux, quality, enthalpy = (coarse[v * ca : (v + 1) * ca] for v in range(3))
        strength = jnp.sqrt(1.0 + flux * flux)
        center = (sections - 1) * jax.nn.sigmoid(enthalpy - 2.0 * quality)
        for base, value in ((0, strength), (2, center)):
            hi, low = split_hi_lo(value)
            for k, part in ((base, hi.astype(F32)), (base + 1, low.astype(F32))):
                for i in range(ca // 2):
                    par[k : k + 1, i * (cb // 2) : (i + 1) * (cb // 2)] = part[2 * i : 2 * i + 1]

        values = par[...].astype(BF16)
        tiled = jnp.concatenate([values] * group, axis=0)

        @pl.loop(0, owners // group)
        def _(b):
            picked = tiled * picks[pl.ds(pl.multiple_of(b * group * 8, group * 8), group * 8)]
            packed = dot_last(picked, in_slot[...]).reshape(group, 8, SLOTS)
            send_buf[pl.ds(b * group, group)] = jnp.concatenate(
                [packed[:, :, :LANES], packed[:, :, LANES:]], axis=1
            ).astype(BF16)

            @pl.loop(0, group)
            def _(k):
                o = b * group + k
                pltpu.make_async_remote_copy(
                    src_ref=send_buf.at[o],
                    dst_ref=recv_buf.at[me],
                    send_sem=row_send.at[o],
                    recv_sem=row_recv.at[me],
                    device_id=(1, o // n_plane, o % n_plane),
                    device_id_type=MESH,
                ).start()

        @pl.loop(0, ca // CHUNK)
        def _(step):
            for t in range(CHUNK):
                a = step * CHUNK + t
                c, _, lap = neighbours(a)
                back = jnp.where(jnp.bitwise_and(col_row, layers - 1) == 0, 0.0, pltpu.roll(c, 1, 0))
                du = c - back
                d, m, q, e = (c[v * layers : (v + 1) * layers] for v in range(4))
                dm, dq, de = (du[v * layers : (v + 1) * layers] for v in (1, 2, 3))
                relaxing = relax_rate / (1.0 + d * d)
                fresh = diffusion * lap + jnp.concatenate(
                    [
                        d - cfl_nozzle * dm,
                        m - cfl_nozzle * (dm + dq),
                        q + relax_step * relaxing * (e - q) - cfl_nozzle * dq,
                        e - cfl_nozzle * de,
                    ],
                    axis=0,
                )
                scatter_row(a, fresh)

        store.start()

        @pl.loop(0, owners)
        def _(o):
            pltpu.make_async_remote_copy(
                src_ref=send_buf.at[o],
                dst_ref=recv_buf.at[me],
                send_sem=row_send.at[o],
                recv_sem=row_recv.at[me],
                device_id=(1, o // n_plane, o % n_plane),
                device_id_type=MESH,
            ).wait_send()

    @pl.when(g == 1)
    def _():
        for copy in spray_args:
            copy.wait()
        folded = jnp.dot(coal_ref[...], fold[...], preferred_element_type=F32).astype(BF16)
        evap = jnp.zeros((sections, cb), F32)
        for k in range(sections):
            evap = jnp.where(col_row == k, evap_ref[k], evap)
        speeds = 0.2 + 0.5 * col_row.astype(F32) / (sections - 1)

        finish_halo()

        @pl.loop(0, ca // CHUNK)
        def _(step):
            parts = []
            for t in range(CHUNK):
                c, up, lap = neighbours(step * CHUNK + t)
                lost = evap * c
                gained = jnp.where(
                    col_row == sections - 1, 0.0, pltpu.roll(lost, sections - 1, 0)
                )
                parts.append(c - speeds * (c - up) + diffusion * lap - lost + gained)
            moved = jnp.concatenate(parts, axis=1)
            first = jnp.dot(folded, pair_terms(moved), preferred_element_type=F32)
            middle = moved + (0.5 * collide_step) * first
            second = jnp.dot(folded, pair_terms(middle), preferred_element_type=F32)
            mixed = moved + collide_step * second
            for t in range(CHUNK):
                scatter_row(step * CHUNK + t, mixed[:, t * cb : (t + 1) * cb])

        level = lax.broadcasted_iota(jnp.int32, (sections, SLOTS), 0).astype(F32)
        index_a = lax.broadcasted_iota(jnp.int32, (ca, SLOTS), 0).astype(F32)
        index_b = lax.broadcasted_iota(jnp.int32, (cb, SLOTS), 0).astype(F32)

        @pl.loop(0, owners // SOURCES)
        def _(step):
            lefts, rights = [], []
            for t in range(SOURCES):
                o = step * SOURCES + t
                pltpu.make_async_remote_copy(
                    src_ref=send_buf.at[o],
                    dst_ref=recv_buf.at[o],
                    send_sem=row_send.at[o],
                    recv_sem=row_recv.at[o],
                    device_id=(0, s, p),
                    device_id_type=MESH,
                ).wait_recv()
                block = recv_buf[o].astype(F32)
                got = jnp.concatenate([block[:8], block[8:]], axis=1)
                strength = got[0:1] + got[1:2]
                center = got[2:3] + got[3:4]
                spread = jnp.full((1, SLOTS), width_ref[0], F32)
                for k in range(1, plumes):
                    spread = jnp.where(got[4:5] == float(k), width_ref[k], spread)
                scaled = (level - center) / spread
                weights = 1.0 / (1.0 + scaled * scaled)
                masses = strength * weights / jnp.sum(weights, axis=0, keepdims=True)
                mask = (got[5:6] == index_a).astype(BF16)
                lefts.append(
                    jnp.concatenate(
                        [
                            jnp.broadcast_to(masses[k : k + 1], (ca, SLOTS)).astype(BF16) * mask
                            for k in range(sections)
                        ],
                        axis=0,
                    )
                )
                rights.append((got[6:7] == index_b).astype(BF16))
            left = jnp.concatenate(lefts, axis=1)
            right = jnp.concatenate(rights, axis=1)
            added = dot_last(left, right)
            tiles = jnp.stack(
                [added[:, h * LANES : (h + 1) * LANES].reshape(rows // 8, 8, LANES) for h in range(2)],
                axis=1,
            )
            obuf[...] += tiles.reshape(2 * rows, LANES)

        store.start()

    store.wait()


def settle(held_hbm, out_hbm, buf, in_sem, out_sem):
    pieces = in_sem.shape[0]
    size = buf.shape[0] // pieces
    parts = [pl.ds(k * size, size) for k in range(pieces)]
    reads = [
        pltpu.make_async_copy(held_hbm.at[at], buf.at[at], in_sem.at[k])
        for k, at in enumerate(parts)
    ]
    writes = [
        pltpu.make_async_copy(buf.at[at], out_hbm.at[at], out_sem.at[k])
        for k, at in enumerate(parts)
    ]
    for read in reads:
        read.start()
    for read, write in zip(reads, writes):
        read.wait()
        write.start()
    for write in writes:
        write.wait()


def body(n_slab, n_plane, fields, evap_rates, coal_kernel, plume_width, owner_map, deposit_cell, plume_ids):
    _, sections, ca, cb = fields.shape
    exit_rows = owner_map.shape[1]
    owners = n_slab * n_plane
    rows = sections * ca
    fold = jnp.asarray(fold_matrix(sections), BF16)
    kept = fold.shape[1]
    hbm = pl.BlockSpec(memory_space=pl.ANY)
    out = pl.pallas_call(
        functools.partial(kernel, n_slab, n_plane, sections, ca, cb, exit_rows),
        out_shape=jax.ShapeDtypeStruct((2 * rows, LANES), F32),
        in_specs=[hbm] * 8,
        out_specs=hbm,
        scratch_shapes=[
            pltpu.VMEM((2 * rows, LANES), F32),
            pltpu.VMEM((ca + 2, sections, cb), F32),
            pltpu.VMEM((2, rows, LANES), F32),
            pltpu.VMEM((2 * rows, LANES), F32),
            pltpu.VMEM((sections * sections, kept), BF16),
            pltpu.VMEM((2, 1, rows), F32),
            pltpu.VMEM((2, 1, rows), F32),
            pltpu.VMEM((8, exit_rows), F32),
            pltpu.VMEM((owners, 16, LANES), BF16),
            pltpu.VMEM((owners, 16, LANES), BF16),
            pltpu.SMEM(evap_rates.shape, F32),
            pltpu.VMEM(coal_kernel.shape, BF16),
            pltpu.SMEM(plume_width.shape, F32),
            pltpu.VMEM((1, exit_rows), jnp.int32),
            pltpu.VMEM((1, exit_rows), jnp.int32),
            pltpu.VMEM((1, exit_rows), jnp.int32),
            pltpu.VMEM((owners * 8, exit_rows), BF16),
            pltpu.VMEM((SLOTS, exit_rows), BF16),
            pltpu.SemaphoreType.DMA,
            pltpu.SemaphoreType.DMA,
            pltpu.SemaphoreType.DMA((4,)),
            pltpu.SemaphoreType.DMA((4,)),
            pltpu.SemaphoreType.DMA((4,)),
            pltpu.SemaphoreType.DMA((owners,)),
            pltpu.SemaphoreType.DMA((owners,)),
        ],
        compiler_params=pltpu.CompilerParams(
            collective_id=0, has_side_effects=True, vmem_limit_bytes=VMEM_BYTES
        ),
    )(
        fields.reshape(rows // 8, 8, 2, LANES).transpose(0, 2, 1, 3).reshape(2 * rows, LANES), evap_rates, coal_kernel, fold, plume_width,
        owner_map, deposit_cell, plume_ids,
    )
    out = pl.pallas_call(
        settle,
        out_shape=jax.ShapeDtypeStruct((2 * rows, LANES), F32),
        in_specs=[hbm],
        out_specs=hbm,
        scratch_shapes=[
            pltpu.VMEM((2 * rows, LANES), F32),
            pltpu.SemaphoreType.DMA((4,)),
            pltpu.SemaphoreType.DMA((4,)),
        ],
        compiler_params=pltpu.CompilerParams(vmem_limit_bytes=VMEM_BYTES),
    )(out)
    out = out.reshape(rows // 8, 2, 8, LANES).transpose(0, 2, 1, 3)
    return out.reshape(1, sections, ca, cb)


def solution(mesh):
    return jax.shard_map(
        functools.partial(body, mesh.shape["slab"], mesh.shape["plane"]),
        mesh=mesh,
        in_specs=(
            P("group", None, "slab", "plane"),
            P(),
            P(),
            P(),
            P(("slab", "plane"), None),
            P(("slab", "plane"), None),
            P(("slab", "plane"), None),
        ),
        out_specs=P("group", None, "slab", "plane"),
        check_vma=False,
    )
```

profile of v0, /device:TPU:5, one launch (start us, length us, event | category | flops | bytes accessed | tf_op | source)
XLA Modules:
  0.0 18.8 jit_solution(13348552324152247992)
XLA Ops:
  0.0 16.8 %shard_map.82.held_hbm = f32[2048,128]{1,0:T(8,128)} custom-call(f32[2048,128]{1,0:T(8,128)} %bitcast.10, f32[32]{0:T(128)} %evap_hbm.1, bf16[32,1024]{1,0:T(8,128)(2,1)} %coal_hbm.1, bf16[1024,640]{1,0:T(8,128)(2,1)} %constant.2.clone.fold_hbm, f32[8]{0:T(128)} %width_hbm.1, s32[1,2048]{1,0:T(1,128)} %owner_hbm.1, s32[1,2048]{1,0:T(1,128)} %cell_hbm.1, ...), custom_call_target="tpu_custom_call" | custom-call | tf_op jit(solution)/shard_map/pallas_call | solution.py:485
  16.8 2.0 %shard_map.83 = f32[2048,128]{1,0:T(8,128)} custom-call(f32[2048,128]{1,0:T(8,128)} %shard_map.82.held_hbm), custom_call_target="tpu_custom_call" | custom-call | tf_op jit(solution)/shard_map/pallas_call | solution.py:524
where the time goes:
time: 19 us; the launch traced here: 18.8 us
  Pallas kernels  18.8 us (99%)
    pallas_call x1, Pallas kernels, body(): pl.pallas_call(functools.partial(kernel, n_slab, n_plane, sections, ca, c...  16.8 us
    pallas_call x1, Pallas kernels, body(): pl.pallas_call(settle, out_shape=jax.ShapeDtypeStruct((2 * rows, LANES),...  1.98 us

commit v1 on v0

--- a/solution.py
+++ b/solution.py
@@ -15,7 +15,8 @@
 SLOTS = 256
 CHUNK = 4
 SOURCES = 4
-VMEM_BYTES = 63 * 1024 * 1024
+PIECES = 4
+VMEM_BYTES = 56 * 1024 * 1024
 
 cfl_nozzle = 0.35
 diffusion = 0.2
@@ -55,14 +56,13 @@
 
 def kernel(
     n_slab, n_plane, sections, ca, cb, exit_rows,
-    fields_hbm, evap_hbm, coal_hbm, fold_hbm, width_hbm, owner_hbm, cell_hbm, pid_hbm,
-    out_hbm,
-    fbuf, tbuf, hbuf, obuf, fold, cols_out, cols_in, par, send_buf, recv_buf,
-    evap_ref, coal_ref, width_ref, owner_ref, cell_ref, pid_ref, picks, in_slot,
-    in_sem, out_sem, arg_sem, halo_send, halo_recv, row_send, row_recv,
+    fields_hbm, evap_hbm, coal_hbm, fold_hbm, owner_hbm, cell_hbm, pid_hbm,
+    obuf, recv_buf,
+    fbuf, tbuf, hbuf, fold, cols_out, cols_in, par, send_buf,
+    evap_ref, coal_ref, owner_ref, cell_ref, pid_ref, picks, in_slot,
+    in_sem, arg_sem, halo_send, halo_recv, row_send, row_recv,
 ):
     owners = n_slab * n_plane
-    plumes = width_ref.shape[0]
     rows = sections * ca
     g = lax.axis_index("group")
     s = lax.axis_index("slab")
@@ -80,7 +80,7 @@
     spray_args = [
         pltpu.make_async_copy(source, target, arg_sem.at[k])
         for k, (source, target) in enumerate(
-            ((evap_hbm, evap_ref), (width_hbm, width_ref), (coal_hbm, coal_ref), (fold_hbm, fold))
+            ((evap_hbm, evap_ref), (coal_hbm, coal_ref), (fold_hbm, fold))
         )
     ]
 
@@ -127,9 +127,6 @@
 
     def half(ref, h):
         return ref[...].reshape(rows // 8, 2, 8, LANES)[:, h].reshape(rows, LANES)
-
-    for a in (0, ca - 1):
-        tbuf[a + 1] = gather_row(fbuf, a)
 
     def halo(kind, target):
         source, landing = (
@@ -147,8 +144,6 @@
             device_id_type=MESH,
         )
 
-    pl.semaphore_wait(barrier, near + jnp.where(g == 0, owners, 0))
-
     outgoing = (sides[1], sides[0], sides[3], sides[2])
     def start_halo(kinds):
         for kind in kinds:
@@ -157,24 +152,25 @@
             def _():
                 halo(kind, outgoing[kind][1]).start()
 
-    start_halo((0, 1))
-
-    lane = lax.broadcasted_iota(jnp.int32, (8, LANES), 1)
-    for h, at in ((0, 0), (1, LANES - 1)):
-        select = (lane == at).astype(BF16)
-        cols_out[h] = dot_last(select, half(fbuf, h).astype(BF16))[0:1]
-
-    start_halo((2, 3))
-
-    @pl.loop(1, ca - 1)
-    def _(a):
-        tbuf[a + 1] = gather_row(fbuf, a)
-
-    for kind, landing in enumerate((tbuf.at[0], tbuf.at[ca + 1], cols_in.at[0], cols_in.at[1])):
-
-        @pl.when(jnp.logical_not(sides[kind][0]))
-        def _():
-            landing[...] = jnp.zeros(landing.shape, F32)
+    def extract_columns():
+        for a in (0, ca - 1):
+            tbuf[a + 1] = gather_row(fbuf, a)
+
+        lane = lax.broadcasted_iota(jnp.int32, (8, LANES), 1)
+        for h, at in ((0, 0), (1, LANES - 1)):
+            select = (lane == at).astype(BF16)
+            cols_out[h] = dot_last(select, half(fbuf, h).astype(BF16))[0:1]
+
+    def fill_rows():
+        @pl.loop(1, ca - 1)
+        def _(a):
+            tbuf[a + 1] = gather_row(fbuf, a)
+
+        for kind, landing in enumerate((tbuf.at[0], tbuf.at[ca + 1], cols_in.at[0], cols_in.at[1])):
+
+            @pl.when(jnp.logical_not(sides[kind][0]))
+            def _():
+                landing[...] = jnp.zeros(landing.shape, F32)
 
     def finish_halo():
         for kind in range(4):
@@ -216,8 +212,6 @@
     def scatter_row(a, value):
         for h in range(2):
             obuf[lines(a, h), :] = value[:, h * LANES : (h + 1) * LANES]
-
-    store = pltpu.make_async_copy(obuf, out_hbm, out_sem)
 
     @pl.when(g == 0)
     def _():
@@ -239,10 +233,12 @@
         cell = cell_ref[...]
         across = jnp.bitwise_and(cell, cb - 1)
         along = jnp.right_shift(cell, cb.bit_length() - 1)
-        par[4:5] = pid_ref[...].astype(F32)
-        par[5:6] = along.astype(F32)
-        par[6:7] = across.astype(F32)
-        par[7:8] = jnp.zeros((1, exit_rows), F32)
+        par[4:5] = (pid_ref[...] * ca + along).astype(F32)
+        par[5:6] = across.astype(F32)
+        number = lax.broadcasted_iota(jnp.int32, (1, exit_rows), 1)
+        half_cb = cb // 2
+        par[6:7] = jnp.bitwise_and(number, half_cb - 1).astype(F32)
+        par[7:8] = (jnp.right_shift(number, half_cb.bit_length() - 1) + 1).astype(F32)
         places = lax.broadcasted_iota(jnp.int32, (SLOTS, exit_rows), 0).astype(F32)
         in_slot[...] = (slot == places).astype(BF16)
         group = 16
@@ -261,8 +257,6 @@
             0.0,
         ).astype(BF16)
 
-        finish_halo()
-
         layers = sections // 4
         plane_row = lax.broadcasted_iota(jnp.int32, (ca, cb), 0)
         plane_lane = lax.broadcasted_iota(jnp.int32, (ca, cb), 1)
@@ -271,16 +265,12 @@
             tiles = fbuf[pl.ds(k * 2 * ca, 2 * ca), :].reshape(ca // 8, 2, 8, LANES)
             return jnp.concatenate([tiles[:, h].reshape(ca, LANES) for h in range(2)], axis=1)
 
-        def plane_lap(c, k):
-            up = jnp.where(plane_row == 0, tbuf[0, k : k + 1], pltpu.roll(c, 1, 0))
-            down = jnp.where(
-                plane_row == ca - 1, tbuf[ca + 1, k : k + 1], pltpu.roll(c, ca - 1, 0)
-            )
+        def plane_lap(c):
+            up = jnp.where(plane_row == 0, 0.0, pltpu.roll(c, 1, 0))
+            down = jnp.where(plane_row == ca - 1, 0.0, pltpu.roll(c, ca - 1, 0))
             left = jnp.where(plane_lane == 0, 0.0, pltpu.roll(c, 1, 1))
             right = jnp.where(plane_lane == cb - 1, 0.0, pltpu.roll(c, cb - 1, 1))
-            at = pl.ds(k * ca, ca)
-            halo_col = jnp.concatenate([hbuf[h, at] for h in range(2)], axis=1)
-            return up + down + (left + right + halo_col) - 4.0 * c
+            return up + down + (left + right) - 4.0 * c
 
         last = [v * layers + layers - 1 for v in range(4)]
         d, m, q, e = (plane(k) for k in last)
@@ -289,30 +279,49 @@
         else:
             dm, dq, de = m, q, e
         relaxing = relax_rate / (1.0 + d * d)
-        exits = [
-            m - cfl_nozzle * (dm + dq) + diffusion * plane_lap(m, last[1]),
-            q
-            + relax_step * relaxing * (e - q)
-            - cfl_nozzle * dq
-            + diffusion * plane_lap(q, last[2]),
-            e - cfl_nozzle * de + diffusion * plane_lap(e, last[3]),
-        ]
-        paired = jnp.concatenate([x + pltpu.roll(x, ca - 1, 0) for x in exits], axis=0)
-        hi = paired.astype(BF16)
-        rest = paired - hi.astype(F32)
+        skew = e - 2.0 * q
+        new_flux = m - cfl_nozzle * (dm + dq) + diffusion * plane_lap(m)
+        new_skew = (
+            skew
+            - cfl_nozzle * (de - 2.0 * dq)
+            - (2.0 * relax_step) * relaxing * (e - q)
+            + diffusion * plane_lap(skew)
+        )
+        planes = jnp.concatenate([new_flux, new_skew, diffusion * m, diffusion * skew], axis=0)
+        paired = planes + pltpu.roll(planes, 4 * ca - 1, 0)
+        edge_rows = jnp.concatenate(
+            [planes[(2 + v) * ca + a : (2 + v) * ca + a + 1] for a in (0, ca - 1) for v in range(2)]
+            + [jnp.zeros((4, cb), F32)],
+            axis=0,
+        )
+        summed = jnp.concatenate([paired[: 2 * ca], edge_rows], axis=0)
+        hi = summed.astype(BF16)
+        rest = summed - hi.astype(F32)
         mid, low = split_hi_lo(rest)
+        count = 2 * ca + 8
         sums = jnp.dot(
             jnp.concatenate([hi, mid, low], axis=0), halve, preferred_element_type=F32
         )
-        coarse = sums[: 3 * ca] + sums[3 * ca : 6 * ca] + sums[6 * ca :]
-        flux, quality, enthalpy = (coarse[v * ca : (v + 1) * ca] for v in range(3))
-        strength = jnp.sqrt(1.0 + flux * flux)
-        center = (sections - 1) * jax.nn.sigmoid(enthalpy - 2.0 * quality)
-        for base, value in ((0, strength), (2, center)):
-            hi, low = split_hi_lo(value)
-            for k, part in ((base, hi.astype(F32)), (base + 1, low.astype(F32))):
+        coarse = sums[:count] + sums[count : 2 * count] + sums[2 * count :]
+        for v in range(2):
+            for k, part in enumerate(split_hi_lo(coarse[v * ca : (v + 1) * ca])):
+                part = part.astype(F32)
                 for i in range(ca // 2):
-                    par[k : k + 1, i * (cb // 2) : (i + 1) * (cb // 2)] = part[2 * i : 2 * i + 1]
+                    par[2 * v + k : 2 * v + k + 1, i * (cb // 2) : (i + 1) * (cb // 2)] = part[
+                        2 * i : 2 * i + 1
+                    ]
+        side_hi, side_lo = split_hi_lo(0.25 * paired[2 * ca :])
+        lane = lax.broadcasted_iota(jnp.int32, (8, cb), 1)
+        line = lax.broadcasted_iota(jnp.int32, (8, cb), 0)
+        ends = jnp.logical_or(
+            jnp.logical_and(line == 0, lane == 0), jnp.logical_and(line == 1, lane == cb - 1)
+        ).astype(BF16)
+        side = dot_last(ends, jnp.concatenate([side_hi, side_lo], axis=0))
+        edge_hi, edge_lo = split_hi_lo(coarse[2 * ca :])
+        edge_hi, edge_lo = edge_hi.astype(F32), edge_lo.astype(F32)
+        edges = jnp.concatenate(
+            [x[n : n + 1] for n in range(4) for x in (edge_hi, edge_lo)] + [side], axis=0
+        ).astype(BF16)
 
         values = par[...].astype(BF16)
         tiled = jnp.concatenate([values] * group, axis=0)
@@ -322,20 +331,32 @@
             picked = tiled * picks[pl.ds(pl.multiple_of(b * group * 8, group * 8), group * 8)]
             packed = dot_last(picked, in_slot[...]).reshape(group, 8, SLOTS)
             send_buf[pl.ds(b * group, group)] = jnp.concatenate(
-                [packed[:, :, :LANES], packed[:, :, LANES:]], axis=1
-            ).astype(BF16)
-
-            @pl.loop(0, group)
-            def _(k):
-                o = b * group + k
-                pltpu.make_async_remote_copy(
-                    src_ref=send_buf.at[o],
-                    dst_ref=recv_buf.at[me],
-                    send_sem=row_send.at[o],
-                    recv_sem=row_recv.at[me],
-                    device_id=(1, o // n_plane, o % n_plane),
-                    device_id_type=MESH,
-                ).start()
+                [
+                    packed[:, :, :LANES].astype(BF16),
+                    packed[:, :, LANES:].astype(BF16),
+                    jnp.broadcast_to(edges[None], (group, 16, LANES)),
+                ],
+                axis=1,
+            )
+
+        pl.semaphore_wait(barrier, near + owners)
+
+        @pl.loop(0, owners)
+        def _(k):
+            o = lax.rem(k + me, owners)
+            pltpu.make_async_remote_copy(
+                src_ref=send_buf.at[o],
+                dst_ref=recv_buf.at[me],
+                send_sem=row_send.at[o],
+                recv_sem=row_recv.at[me],
+                device_id=(1, o // n_plane, o % n_plane),
+                device_id_type=MESH,
+            ).start()
+
+        extract_columns()
+        start_halo((0, 1, 2, 3))
+        fill_rows()
+        finish_halo()
 
         @pl.loop(0, ca // CHUNK)
         def _(step):
@@ -358,8 +379,6 @@
                 )
                 scatter_row(a, fresh)
 
-        store.start()
-
         @pl.loop(0, owners)
         def _(o):
             pltpu.make_async_remote_copy(
@@ -373,6 +392,10 @@
 
     @pl.when(g == 1)
     def _():
+        extract_columns()
+        pl.semaphore_wait(barrier, near)
+        start_halo((0, 1, 2, 3))
+        fill_rows()
         for copy in spray_args:
             copy.wait()
         folded = jnp.dot(coal_ref[...], fold[...], preferred_element_type=F32).astype(BF16)
@@ -401,77 +424,138 @@
             for t in range(CHUNK):
                 scatter_row(step * CHUNK + t, mixed[:, t * cb : (t + 1) * cb])
 
+        @pl.loop(0, owners)
+        def _(o):
+            pltpu.make_async_remote_copy(
+                src_ref=send_buf.at[o],
+                dst_ref=recv_buf.at[o],
+                send_sem=row_send.at[o],
+                recv_sem=row_recv.at[o],
+                device_id=(0, s, p),
+                device_id_type=MESH,
+            ).wait_recv()
+
+
+def finish(
+    n_plane, owners, sections, ca, cb,
+    held, rows_in, width_hbm,
+    out_hbm,
+    obuf, flat, par, mass, right, mask, width_ref, arg_sem, out_sem,
+):
+    plumes = width_ref.shape[0]
+    rows = sections * ca
+    g = lax.axis_index("group")
+
+    @pl.when(g == 0)
+    def _():
+        copy = pltpu.make_async_copy(held, out_hbm, out_sem.at[0])
+        copy.start()
+        copy.wait()
+
+    @pl.when(g == 1)
+    def _():
+        fetch = pltpu.make_async_copy(width_hbm, width_ref, arg_sem)
+        fetch.start()
+        pad = n_plane * 32
+        half_cb = cb // 2
+        flat[pl.ds(0, pad)] = jnp.zeros((pad, LANES), F32)
+        flat[pl.ds(pad + owners * 32, pad)] = jnp.zeros((pad, LANES), F32)
+
+        @pl.loop(0, owners // 8)
+        def _(b):
+            at = pl.ds(pl.multiple_of(pad + b * 256, 128), 256)
+            flat[at] = rows_in[pl.ds(b * 8, 8)].astype(F32).reshape(256, LANES)
+
+        fetch.wait()
+        sub = lax.broadcasted_iota(jnp.int32, (8, LANES), 0)
+
+        @pl.loop(0, owners // 8)
+        def _(b):
+            def take(shift, line):
+                return flat[pl.ds(pad + (b * 8 + shift) * 32 + line, 8, stride=32), :]
+
+            plane_at = lax.rem(b * 8 + sub, n_plane)
+            first_plane = plane_at == 0
+            last_plane = plane_at == n_plane - 1
+            above = [take(-n_plane, 16 + 4 + x) for x in range(4)]
+            below = [take(n_plane, 16 + x) for x in range(4)]
+            before = jnp.where(first_plane, 0.0, take(-1, 16 + 9))
+            behind = jnp.where(last_plane, 0.0, take(1, 16 + 8))
+
+            def pick(table, index):
+                return jnp.take_along_axis(table, index, axis=1, mode="promise_in_bounds")
+
+            for h in range(2):
+                got = [take(0, h * 8 + x) for x in range(8)]
+                spot = got[6].astype(jnp.int32)
+                line = got[7].astype(jnp.int32)
+                slot_line = 2 * jnp.maximum(line - 1, 0)
+                flux = got[0] + got[1]
+                skew = got[2] + got[3]
+                for tables, here in ((above, line == 1), (below, line == ca // 2)):
+                    f0, f1, u0, u1 = (pick(table, spot) for table in tables)
+                    flux += jnp.where(here, f0 + f1, 0.0)
+                    skew += jnp.where(here, u0 + u1, 0.0)
+                for table, here in ((before, spot == 0), (behind, spot == half_cb - 1)):
+                    f0, u0, f1, u1 = (pick(table, slot_line + ca * x) for x in range(4))
+                    flux += jnp.where(here, f0 + f1, 0.0)
+                    skew += jnp.where(here, u0 + u1, 0.0)
+                code = got[4].astype(jnp.int32)
+                plume = jnp.right_shift(code, ca.bit_length() - 1)
+                spread = jnp.full((8, LANES), width_ref[0], F32)
+                for k in range(1, plumes):
+                    spread = jnp.where(plume == k, width_ref[k], spread)
+                values = (
+                    jnp.where(line > 0, jnp.sqrt(1.0 + flux * flux), 0.0),
+                    (sections - 1) * jax.nn.sigmoid(skew),
+                    1.0 / spread,
+                    jnp.bitwise_and(code, ca - 1).astype(F32),
+                    got[5],
+                )
+                for x, value in enumerate(values):
+                    par[x, pl.ds(pl.multiple_of(b * 8, 8), 8), h * LANES : (h + 1) * LANES] = value
+
         level = lax.broadcasted_iota(jnp.int32, (sections, SLOTS), 0).astype(F32)
         index_a = lax.broadcasted_iota(jnp.int32, (ca, SLOTS), 0).astype(F32)
         index_b = lax.broadcasted_iota(jnp.int32, (cb, SLOTS), 0).astype(F32)
 
         @pl.loop(0, owners // SOURCES)
         def _(step):
-            lefts, rights = [], []
             for t in range(SOURCES):
                 o = step * SOURCES + t
-                pltpu.make_async_remote_copy(
-                    src_ref=send_buf.at[o],
-                    dst_ref=recv_buf.at[o],
-                    send_sem=row_send.at[o],
-                    recv_sem=row_recv.at[o],
-                    device_id=(0, s, p),
-                    device_id_type=MESH,
-                ).wait_recv()
-                block = recv_buf[o].astype(F32)
-                got = jnp.concatenate([block[:8], block[8:]], axis=1)
-                strength = got[0:1] + got[1:2]
-                center = got[2:3] + got[3:4]
-                spread = jnp.full((1, SLOTS), width_ref[0], F32)
-                for k in range(1, plumes):
-                    spread = jnp.where(got[4:5] == float(k), width_ref[k], spread)
-                scaled = (level - center) / spread
+                strength, center, inverse, along, across = (
+                    par[x, pl.ds(o, 1), :] for x in range(5)
+                )
+                scaled = (level - center) * inverse
                 weights = 1.0 / (1.0 + scaled * scaled)
-                masses = strength * weights / jnp.sum(weights, axis=0, keepdims=True)
-                mask = (got[5:6] == index_a).astype(BF16)
-                lefts.append(
-                    jnp.concatenate(
-                        [
-                            jnp.broadcast_to(masses[k : k + 1], (ca, SLOTS)).astype(BF16) * mask
-                            for k in range(sections)
-                        ],
-                        axis=0,
-                    )
-                )
-                rights.append((got[6:7] == index_b).astype(BF16))
-            left = jnp.concatenate(lefts, axis=1)
-            right = jnp.concatenate(rights, axis=1)
-            added = dot_last(left, right)
+                at = pl.ds(t * SLOTS, SLOTS)
+                mass[:, at] = weights * (strength / jnp.sum(weights, axis=0, keepdims=True))
+                mask[:, at] = (along == index_a).astype(BF16)
+                right[:, at] = (across == index_b).astype(BF16)
+            left = jnp.concatenate(
+                [
+                    jnp.broadcast_to(mass[k : k + 1], (ca, SOURCES * SLOTS)).astype(BF16) * mask[...]
+                    for k in range(sections)
+                ],
+                axis=0,
+            )
+            added = dot_last(left, right[...])
             tiles = jnp.stack(
                 [added[:, h * LANES : (h + 1) * LANES].reshape(rows // 8, 8, LANES) for h in range(2)],
                 axis=1,
-            )
-            obuf[...] += tiles.reshape(2 * rows, LANES)
-
+            ).reshape(2 * rows, LANES)
+
+            @pl.when(step == 0)
+            def _():
+                obuf[...] = held[...] + tiles
+
+            @pl.when(step > 0)
+            def _():
+                obuf[...] += tiles
+
+        store = pltpu.make_async_copy(obuf, out_hbm, out_sem.at[0])
         store.start()
-
-    store.wait()
-
-
-def settle(held_hbm, out_hbm, buf, in_sem, out_sem):
-    pieces = in_sem.shape[0]
-    size = buf.shape[0] // pieces
-    parts = [pl.ds(k * size, size) for k in range(pieces)]
-    reads = [
-        pltpu.make_async_copy(held_hbm.at[at], buf.at[at], in_sem.at[k])
-        for k, at in enumerate(parts)
-    ]
-    writes = [
-        pltpu.make_async_copy(buf.at[at], out_hbm.at[at], out_sem.at[k])
-        for k, at in enumerate(parts)
-    ]
-    for read in reads:
-        read.start()
-    for read, write in zip(reads, writes):
-        read.wait()
-        write.start()
-    for write in writes:
-        write.wait()
+        store.wait()
 
 
 def body(n_slab, n_plane, fields, evap_rates, coal_kernel, plume_width, owner_map, deposit_cell, plume_ids):
@@ -482,31 +566,31 @@
     fold = jnp.asarray(fold_matrix(sections), BF16)
     kept = fold.shape[1]
     hbm = pl.BlockSpec(memory_space=pl.ANY)
-    out = pl.pallas_call(
+    vmem = pl.BlockSpec(memory_space=pltpu.VMEM)
+    held, rows_in = pl.pallas_call(
         functools.partial(kernel, n_slab, n_plane, sections, ca, cb, exit_rows),
-        out_shape=jax.ShapeDtypeStruct((2 * rows, LANES), F32),
-        in_specs=[hbm] * 8,
-        out_specs=hbm,
+        out_shape=[
+            pltpu.VMEM((2 * rows, LANES), F32),
+            pltpu.VMEM((owners, 32, LANES), BF16),
+        ],
+        in_specs=[hbm] * 7,
+        out_specs=[vmem] * 2,
         scratch_shapes=[
             pltpu.VMEM((2 * rows, LANES), F32),
             pltpu.VMEM((ca + 2, sections, cb), F32),
             pltpu.VMEM((2, rows, LANES), F32),
-            pltpu.VMEM((2 * rows, LANES), F32),
             pltpu.VMEM((sections * sections, kept), BF16),
             pltpu.VMEM((2, 1, rows), F32),
             pltpu.VMEM((2, 1, rows), F32),
             pltpu.VMEM((8, exit_rows), F32),
-            pltpu.VMEM((owners, 16, LANES), BF16),
-            pltpu.VMEM((owners, 16, LANES), BF16),
+            pltpu.VMEM((owners, 32, LANES), BF16),
             pltpu.SMEM(evap_rates.shape, F32),
             pltpu.VMEM(coal_kernel.shape, BF16),
-            pltpu.SMEM(plume_width.shape, F32),
             pltpu.VMEM((1, exit_rows), jnp.int32),
             pltpu.VMEM((1, exit_rows), jnp.int32),
             pltpu.VMEM((1, exit_rows), jnp.int32),
             pltpu.VMEM((owners * 8, exit_rows), BF16),
             pltpu.VMEM((SLOTS, exit_rows), BF16),
-            pltpu.SemaphoreType.DMA,
             pltpu.SemaphoreType.DMA,
             pltpu.SemaphoreType.DMA((4,)),
             pltpu.SemaphoreType.DMA((4,)),
@@ -518,21 +602,32 @@
             collective_id=0, has_side_effects=True, vmem_limit_bytes=VMEM_BYTES
         ),
     )(
-        fields.reshape(rows // 8, 8, 2, LANES).transpose(0, 2, 1, 3).reshape(2 * rows, LANES), evap_rates, coal_kernel, fold, plume_width,
+        fields.reshape(rows // 8, 8, 2, LANES).transpose(0, 2, 1, 3).reshape(2 * rows, LANES), evap_rates, coal_kernel, fold,
         owner_map, deposit_cell, plume_ids,
     )
+    span = SOURCES * SLOTS
     out = pl.pallas_call(
-        settle,
+        functools.partial(finish, n_plane, owners, sections, ca, cb),
         out_shape=jax.ShapeDtypeStruct((2 * rows, LANES), F32),
-        in_specs=[hbm],
+        in_specs=[vmem, vmem, hbm],
         out_specs=hbm,
         scratch_shapes=[
             pltpu.VMEM((2 * rows, LANES), F32),
-            pltpu.SemaphoreType.DMA((4,)),
-            pltpu.SemaphoreType.DMA((4,)),
+            pltpu.VMEM(((owners + 2 * n_plane) * 32, LANES), F32),
+            pltpu.VMEM((5, owners, SLOTS), F32),
+            pltpu.VMEM((sections, span), F32),
+            pltpu.VMEM((cb, span), BF16),
+            pltpu.VMEM((ca, span), BF16),
+            pltpu.SMEM(plume_width.shape, F32),
+            pltpu.SemaphoreType.DMA,
+            pltpu.SemaphoreType.DMA((PIECES,)),
         ],
         compiler_params=pltpu.CompilerParams(vmem_limit_bytes=VMEM_BYTES),
-    )(out)
+    )(
+        pltpu.with_memory_space_constraint(held, pltpu.VMEM),
+        pltpu.with_memory_space_constraint(rows_in, pltpu.VMEM),
+        plume_width,
+    )
     out = out.reshape(rows // 8, 2, 8, LANES).transpose(0, 2, 1, 3)
     return out.reshape(1, sections, ca, cb)
 

time: 19 us -> 17.4 us (0.916)
  the two profiles are of different devices: /device:TPU:5 before, /device:TPU:14 now
where the time goes in v1:
time: 17.4 us; the launch traced here: 17.2 us
  Pallas kernels  17.2 us (99%)
    pallas_call x1, Pallas kernels, body(): pl.pallas_call(functools.partial(kernel, n_slab, n_plane, sections, ca, c...  11.7 us
    pallas_call x1, Pallas kernels, body(): pl.pallas_call(functools.partial(finish, n_plane, owners, sections, ca, c...  5.53 us

profile of v1, /device:TPU:14, one launch (start us, length us, event | category | flops | bytes accessed | tf_op | source)
XLA Modules:
  0.0 17.2 jit_solution(16759882142468956690)
XLA Ops:
  0.0 11.7 %shard_map.82 = (f32[2048,128]{1,0:T(8,128)S(1)}, bf16[16,32,128]{2,1,0:T(8,128)(2,1)S(1)}) custom-call(f32[2048,128]{1,0:T(8,128)} %bitcast.10, f32[32]{0:T(128)} %evap_hbm.1, bf16[32,1024]{1,0:T(8,128)(2,1)} %coal_hbm.1, bf16[1024,640]{1,0:T(8,128)(2,1)} %constant.2.clone.fold_hbm, s32[1,2048]{1,0:T(1,128)} %owner_hbm.1, s32[1,2048]{1,0:T(1,128)} %cell_hbm.1, ...), custom_call_target="tpu_custom_call" | custom-call | tf_op jit(solution)/shard_map/pallas_call | solution.py:570
  11.7 5.5 %shard_map.83 = f32[2048,128]{1,0:T(8,128)} custom-call(f32[2048,128]{1,0:T(8,128)S(1)} %get-tuple-element.7.held, bf16[16,32,128]{2,1,0:T(8,128)(2,1)S(1)} %get-tuple-element.8.rows_in, f32[8]{0:T(128)} %width_hbm.1), custom_call_target="tpu_custom_call" | custom-call | tf_op jit(solution)/shard_map/pallas_call | solution.py:609

commit v2 on v1

--- a/solution.py
+++ b/solution.py
@@ -14,8 +14,9 @@
 LANES = 128
 SLOTS = 256
 CHUNK = 4
+PAD = 8
 SOURCES = 4
-PIECES = 4
+PIECES = 2
 VMEM_BYTES = 56 * 1024 * 1024
 
 cfl_nozzle = 0.35
@@ -58,7 +59,7 @@
     n_slab, n_plane, sections, ca, cb, exit_rows,
     fields_hbm, evap_hbm, coal_hbm, fold_hbm, owner_hbm, cell_hbm, pid_hbm,
     obuf, recv_buf,
-    fbuf, tbuf, hbuf, fold, cols_out, cols_in, par, send_buf,
+    fbuf, tbuf, edge_in, hbuf, fold, cols_out, cols_in, par, send_buf,
     evap_ref, coal_ref, owner_ref, cell_ref, pid_ref, picks, in_slot,
     in_sem, arg_sem, halo_send, halo_recv, row_send, row_recv,
 ):
@@ -69,7 +70,11 @@
     p = lax.axis_index("plane")
     me = s * n_plane + p
 
-    load = pltpu.make_async_copy(fields_hbm, fbuf, in_sem)
+    fpad = fbuf.reshape(sections, 2 * ca + PAD, LANES).at[:, pl.ds(0, 2 * ca), :]
+    opad = obuf.reshape(sections, 2 * ca + PAD, LANES).at[:, pl.ds(0, 2 * ca), :]
+    load = pltpu.make_async_copy(
+        fields_hbm.reshape(sections, 2 * ca, LANES), fpad, in_sem
+    )
     load.start()
     nozzle_args = [
         pltpu.make_async_copy(source, target, arg_sem.at[k])
@@ -120,7 +125,7 @@
     load.wait()
 
     def lines(a, h):
-        return pl.ds(a // 8 * 16 + h * 8 + a % 8, sections, stride=2 * ca)
+        return pl.ds(a // 8 * 16 + h * 8 + a % 8, sections, stride=2 * ca + PAD)
 
     def gather_row(ref, a):
         return jnp.concatenate([ref[lines(a, h), :] for h in range(2)], axis=1)
@@ -130,8 +135,8 @@
 
     def halo(kind, target):
         source, landing = (
-            (tbuf.at[ca], tbuf.at[0]),
-            (tbuf.at[1], tbuf.at[ca + 1]),
+            (tbuf.at[ca], edge_in.at[0]),
+            (tbuf.at[1], edge_in.at[1]),
             (cols_out.at[1], cols_in.at[0]),
             (cols_out.at[0], cols_in.at[1]),
         )[kind]
@@ -159,20 +164,20 @@
         lane = lax.broadcasted_iota(jnp.int32, (8, LANES), 1)
         for h, at in ((0, 0), (1, LANES - 1)):
             select = (lane == at).astype(BF16)
-            cols_out[h] = dot_last(select, half(fbuf, h).astype(BF16))[0:1]
+            cols_out[h] = dot_last(select, half(fpad, h).astype(BF16))[0:1]
 
     def fill_rows():
         @pl.loop(1, ca - 1)
         def _(a):
             tbuf[a + 1] = gather_row(fbuf, a)
 
-        for kind, landing in enumerate((tbuf.at[0], tbuf.at[ca + 1], cols_in.at[0], cols_in.at[1])):
+        for kind, landing in enumerate((edge_in.at[0], edge_in.at[1], cols_in.at[0], cols_in.at[1])):
 
             @pl.when(jnp.logical_not(sides[kind][0]))
             def _():
                 landing[...] = jnp.zeros(landing.shape, F32)
 
-    def finish_halo():
+    def wait_halo():
         for kind in range(4):
 
             @pl.when(outgoing[kind][0])
@@ -183,30 +188,32 @@
             def _():
                 halo(kind, outgoing[kind][1]).wait_recv()
 
+    def placed_columns():
         sub = lax.broadcasted_iota(jnp.int32, (16, cb), 0)
         lanes = lax.broadcasted_iota(jnp.int32, (16, cb), 1)
         stack = jnp.concatenate([cols_in[0], cols_in[1], jnp.zeros((14, rows), F32)], axis=0)
         place = jnp.logical_or(
             jnp.logical_and(sub == 0, lanes == 0), jnp.logical_and(sub == 1, lanes == cb - 1)
         ).astype(BF16)
-        placed = jnp.dot(stack.T.astype(BF16), place, preferred_element_type=F32)
-        for h in range(2):
-            hbuf[h] = placed[:, h * LANES : (h + 1) * LANES]
+        return jnp.dot(stack.T.astype(BF16), place, preferred_element_type=F32)
 
     col_lane = lax.broadcasted_iota(jnp.int32, (sections, cb), 1)
     col_row = lax.broadcasted_iota(jnp.int32, (sections, cb), 0)
 
     def column_halo(a):
         return jnp.concatenate(
-            [hbuf[h, pl.ds(a, sections, stride=ca), :] for h in range(2)], axis=1
+            [hbuf[h, pl.ds(a, sections, stride=ca + PAD), :] for h in range(2)], axis=1
         )
 
-    def neighbours(a):
+    def neighbours(a, with_columns):
         c = tbuf[a + 1]
         up = tbuf[a]
         left = jnp.where(col_lane == 0, 0.0, pltpu.roll(c, 1, 1))
         right = jnp.where(col_lane == cb - 1, 0.0, pltpu.roll(c, cb - 1, 1))
-        lap = up + tbuf[a + 2] + (left + right + column_halo(a)) - 4.0 * c
+        beside = left + right
+        if with_columns:
+            beside += column_halo(a)
+        lap = up + tbuf[a + 2] + beside - 4.0 * c
         return c, up, lap
 
     def scatter_row(a, value):
@@ -262,7 +269,7 @@
         plane_lane = lax.broadcasted_iota(jnp.int32, (ca, cb), 1)
 
         def plane(k):
-            tiles = fbuf[pl.ds(k * 2 * ca, 2 * ca), :].reshape(ca // 8, 2, 8, LANES)
+            tiles = fbuf[pl.ds(k * (2 * ca + PAD), 2 * ca), :].reshape(ca // 8, 2, 8, LANES)
             return jnp.concatenate([tiles[:, h].reshape(ca, LANES) for h in range(2)], axis=1)
 
         def plane_lap(c):
@@ -356,13 +363,14 @@
         extract_columns()
         start_halo((0, 1, 2, 3))
         fill_rows()
-        finish_halo()
+        for a in (0, ca + 1):
+            tbuf[a] = jnp.zeros((sections, cb), F32)
 
         @pl.loop(0, ca // CHUNK)
         def _(step):
             for t in range(CHUNK):
                 a = step * CHUNK + t
-                c, _, lap = neighbours(a)
+                c, _, lap = neighbours(a, False)
                 back = jnp.where(jnp.bitwise_and(col_row, layers - 1) == 0, 0.0, pltpu.roll(c, 1, 0))
                 du = c - back
                 d, m, q, e = (c[v * layers : (v + 1) * layers] for v in range(4))
@@ -379,6 +387,16 @@
                 )
                 scatter_row(a, fresh)
 
+        wait_halo()
+        placed = diffusion * placed_columns()
+        opad[...] += jnp.stack(
+            [placed[:, h * LANES : (h + 1) * LANES].reshape(rows // 8, 8, LANES) for h in range(2)],
+            axis=1,
+        ).reshape(sections, 2 * ca, LANES)
+        for side, a in enumerate((0, ca - 1)):
+            for h in range(2):
+                obuf[lines(a, h), :] += diffusion * edge_in[side, :, h * LANES : (h + 1) * LANES]
+
         @pl.loop(0, owners)
         def _(o):
             pltpu.make_async_remote_copy(
@@ -404,13 +422,20 @@
             evap = jnp.where(col_row == k, evap_ref[k], evap)
         speeds = 0.2 + 0.5 * col_row.astype(F32) / (sections - 1)
 
-        finish_halo()
+        wait_halo()
+        for side, a in enumerate((0, ca + 1)):
+            tbuf[a] = edge_in[side]
+        placed = placed_columns()
+        for h in range(2):
+            hbuf.reshape(2, sections, ca + PAD, LANES)[h, :, pl.ds(0, ca), :] = placed[
+                :, h * LANES : (h + 1) * LANES
+            ].reshape(sections, ca, LANES)
 
         @pl.loop(0, ca // CHUNK)
         def _(step):
             parts = []
             for t in range(CHUNK):
-                c, up, lap = neighbours(step * CHUNK + t)
+                c, up, lap = neighbours(step * CHUNK + t, True)
                 lost = evap * c
                 gained = jnp.where(
                     col_row == sections - 1, 0.0, pltpu.roll(lost, sections - 1, 0)
@@ -440,15 +465,17 @@
     n_plane, owners, sections, ca, cb,
     held, rows_in, width_hbm,
     out_hbm,
-    obuf, flat, par, mass, right, mask, width_ref, arg_sem, out_sem,
+    obuf, flat, par, mass, left_even, left_odd, right_even, right_odd, width_ref, arg_sem, out_sem,
 ):
     plumes = width_ref.shape[0]
     rows = sections * ca
     g = lax.axis_index("group")
+    whole = held.reshape(sections, 2 * ca + PAD, LANES).at[:, pl.ds(0, 2 * ca), :]
+    out_whole = out_hbm.reshape(sections, 2 * ca, LANES)
 
     @pl.when(g == 0)
     def _():
-        copy = pltpu.make_async_copy(held, out_hbm, out_sem.at[0])
+        copy = pltpu.make_async_copy(whole, out_whole, out_sem.at[0])
         copy.start()
         copy.wait()
 
@@ -456,6 +483,8 @@
     def _():
         fetch = pltpu.make_async_copy(width_hbm, width_ref, arg_sem)
         fetch.start()
+        fill = pltpu.make_async_copy(whole, obuf, out_sem.at[PIECES])
+        fill.start()
         pad = n_plane * 32
         half_cb = cb // 2
         flat[pl.ds(0, pad)] = jnp.zeros((pad, LANES), F32)
@@ -515,47 +544,63 @@
                 for x, value in enumerate(values):
                     par[x, pl.ds(pl.multiple_of(b * 8, 8), 8), h * LANES : (h + 1) * LANES] = value
 
-        level = lax.broadcasted_iota(jnp.int32, (sections, SLOTS), 0).astype(F32)
-        index_a = lax.broadcasted_iota(jnp.int32, (ca, SLOTS), 0).astype(F32)
-        index_b = lax.broadcasted_iota(jnp.int32, (cb, SLOTS), 0).astype(F32)
-
-        @pl.loop(0, owners // SOURCES)
-        def _(step):
-            for t in range(SOURCES):
-                o = step * SOURCES + t
-                strength, center, inverse, along, across = (
-                    par[x, pl.ds(o, 1), :] for x in range(5)
+        span = SOURCES * SLOTS
+        level = lax.broadcasted_iota(jnp.int32, (sections, span), 0).astype(F32)
+        index_a = lax.broadcasted_iota(jnp.int32, (ca, span), 0).astype(F32)
+        index_b = lax.broadcasted_iota(jnp.int32, (cb, span), 0).astype(F32)
+
+        def build(step, left, right):
+            strength, center, inverse, along, across = (
+                jnp.concatenate(
+                    [par[x, pl.ds(step * SOURCES + t, 1), :] for t in range(SOURCES)], axis=1
                 )
-                scaled = (level - center) * inverse
-                weights = 1.0 / (1.0 + scaled * scaled)
-                at = pl.ds(t * SLOTS, SLOTS)
-                mass[:, at] = weights * (strength / jnp.sum(weights, axis=0, keepdims=True))
-                mask[:, at] = (along == index_a).astype(BF16)
-                right[:, at] = (across == index_b).astype(BF16)
-            left = jnp.concatenate(
+                for x in range(5)
+            )
+            scaled = (level - center) * inverse
+            weights = 1.0 / (1.0 + scaled * scaled)
+            mass[...] = weights * (strength / jnp.sum(weights, axis=0, keepdims=True))
+            mask = (along == index_a).astype(BF16)
+            right[...] = (across == index_b).astype(BF16)
+            for k in range(sections):
+                left[k * ca : (k + 1) * ca] = (
+                    jnp.broadcast_to(mass[k : k + 1], (ca, span)).astype(BF16) * mask
+                )
+
+        def add(left, right, first, count):
+            added = dot_last(left[first * ca : (first + count) * ca], right[...])
+            tiles = jnp.stack(
                 [
-                    jnp.broadcast_to(mass[k : k + 1], (ca, SOURCES * SLOTS)).astype(BF16) * mask[...]
-                    for k in range(sections)
+                    added[:, h * LANES : (h + 1) * LANES].reshape(count * ca // 8, 8, LANES)
+                    for h in range(2)
                 ],
-                axis=0,
+                axis=1,
             )
-            added = dot_last(left, right[...])
-            tiles = jnp.stack(
-                [added[:, h * LANES : (h + 1) * LANES].reshape(rows // 8, 8, LANES) for h in range(2)],
-                axis=1,
-            ).reshape(2 * rows, LANES)
-
-            @pl.when(step == 0)
-            def _():
-                obuf[...] = held[...] + tiles
-
-            @pl.when(step > 0)
-            def _():
-                obuf[...] += tiles
-
-        store = pltpu.make_async_copy(obuf, out_hbm, out_sem.at[0])
-        store.start()
-        store.wait()
+            obuf[first : first + count] += tiles.reshape(count, 2 * ca, LANES)
+
+        build(0, left_even, right_even)
+        fill.wait()
+        steps = owners // SOURCES
+
+        @pl.loop(0, steps // 2 - 1)
+        def _(i):
+            add(left_even, right_even, 0, sections)
+            build(2 * i + 1, left_odd, right_odd)
+            add(left_odd, right_odd, 0, sections)
+            build(2 * i + 2, left_even, right_even)
+
+        add(left_even, right_even, 0, sections)
+        build(steps - 1, left_odd, right_odd)
+        each = sections // PIECES
+        stores = []
+        for c in range(PIECES):
+            add(left_odd, right_odd, c * each, each)
+            at = pl.ds(c * each, each)
+            stores.append(
+                pltpu.make_async_copy(obuf.at[at], out_whole.at[at], out_sem.at[c])
+            )
+            stores[-1].start()
+        for store in stores:
+            store.wait()
 
 
 def body(n_slab, n_plane, fields, evap_rates, coal_kernel, plume_width, owner_map, deposit_cell, plume_ids):
@@ -570,15 +615,16 @@
     held, rows_in = pl.pallas_call(
         functools.partial(kernel, n_slab, n_plane, sections, ca, cb, exit_rows),
         out_shape=[
-            pltpu.VMEM((2 * rows, LANES), F32),
+            pltpu.VMEM((2 * rows + sections * PAD, LANES), F32),
             pltpu.VMEM((owners, 32, LANES), BF16),
         ],
         in_specs=[hbm] * 7,
         out_specs=[vmem] * 2,
         scratch_shapes=[
-            pltpu.VMEM((2 * rows, LANES), F32),
+            pltpu.VMEM((2 * rows + sections * PAD, LANES), F32),
             pltpu.VMEM((ca + 2, sections, cb), F32),
-            pltpu.VMEM((2, rows, LANES), F32),
+            pltpu.VMEM((2, sections, cb), F32),
+            pltpu.VMEM((2, rows + sections * PAD, LANES), F32),
             pltpu.VMEM((sections * sections, kept), BF16),
             pltpu.VMEM((2, 1, rows), F32),
             pltpu.VMEM((2, 1, rows), F32),
@@ -612,15 +658,17 @@
         in_specs=[vmem, vmem, hbm],
         out_specs=hbm,
         scratch_shapes=[
-            pltpu.VMEM((2 * rows, LANES), F32),
+            pltpu.VMEM((sections, 2 * ca, LANES), F32),
             pltpu.VMEM(((owners + 2 * n_plane) * 32, LANES), F32),
             pltpu.VMEM((5, owners, SLOTS), F32),
             pltpu.VMEM((sections, span), F32),
+            pltpu.VMEM((rows, span), BF16),
+            pltpu.VMEM((rows, span), BF16),
             pltpu.VMEM((cb, span), BF16),
-            pltpu.VMEM((ca, span), BF16),
+            pltpu.VMEM((cb, span), BF16),
             pltpu.SMEM(plume_width.shape, F32),
             pltpu.SemaphoreType.DMA,
-            pltpu.SemaphoreType.DMA((PIECES,)),
+            pltpu.SemaphoreType.DMA((PIECES + 1,)),
         ],
         compiler_params=pltpu.CompilerParams(vmem_limit_bytes=VMEM_BYTES),
     )(

time: 17.4 us -> 16.1 us (0.925)
  the two profiles are of different devices: /device:TPU:14 before, /device:TPU:6 now
where the time goes in v2:
time: 16.1 us; the launch traced here: 15.9 us
  Pallas kernels  15.9 us (99%)
    pallas_call x1, Pallas kernels, body(): pl.pallas_call(functools.partial(kernel, n_slab, n_plane, sections, ca, c...  11.2 us
    pallas_call x1, Pallas kernels, body(): pl.pallas_call(functools.partial(finish, n_plane, owners, sections, ca, c...  4.7 us

profile of v2, /device:TPU:6, one launch (start us, length us, event | category | flops | bytes accessed | tf_op | source)
XLA Modules:
  0.0 15.9 jit_solution(17303305376019201298)
XLA Ops:
  0.0 11.2 %shard_map.82 = (f32[2304,128]{1,0:T(8,128)S(1)}, bf16[16,32,128]{2,1,0:T(8,128)(2,1)S(1)}) custom-call(f32[2048,128]{1,0:T(8,128)} %bitcast.10, f32[32]{0:T(128)} %evap_hbm.1, bf16[32,1024]{1,0:T(8,128)(2,1)} %coal_hbm.1, bf16[1024,640]{1,0:T(8,128)(2,1)} %constant.2.clone.fold_hbm, s32[1,2048]{1,0:T(1,128)} %owner_hbm.1, s32[1,2048]{1,0:T(1,128)} %cell_hbm.1, ...), custom_call_target="tpu_custom_call" | custom-call | tf_op jit(solution)/shard_map/pallas_call | solution.py:615
  11.2 4.7 %shard_map.83 = f32[2048,128]{1,0:T(8,128)} custom-call(f32[2304,128]{1,0:T(8,128)S(1)} %get-tuple-element.7.held, bf16[16,32,128]{2,1,0:T(8,128)(2,1)S(1)} %get-tuple-element.8.rows_in, f32[8]{0:T(128)} %width_hbm.1), custom_call_target="tpu_custom_call" | custom-call | tf_op jit(solution)/shard_map/pallas_call | solution.py:655

commit v3 on v2

--- a/solution.py
+++ b/solution.py
@@ -13,7 +13,7 @@
 BF16 = jnp.bfloat16
 LANES = 128
 SLOTS = 256
-CHUNK = 4
+CHUNK = 8
 PAD = 8
 SOURCES = 4
 PIECES = 2
@@ -350,7 +350,7 @@
 
         @pl.loop(0, owners)
         def _(k):
-            o = lax.rem(k + me, owners)
+            o = jnp.where(2 * s < n_slab, owners - 1 - k, k)
             pltpu.make_async_remote_copy(
                 src_ref=send_buf.at[o],
                 dst_ref=recv_buf.at[me],
@@ -441,13 +441,21 @@
                     col_row == sections - 1, 0.0, pltpu.roll(lost, sections - 1, 0)
                 )
                 parts.append(c - speeds * (c - up) + diffusion * lap - lost + gained)
-            moved = jnp.concatenate(parts, axis=1)
-            first = jnp.dot(folded, pair_terms(moved), preferred_element_type=F32)
-            middle = moved + (0.5 * collide_step) * first
-            second = jnp.dot(folded, pair_terms(middle), preferred_element_type=F32)
-            mixed = moved + collide_step * second
-            for t in range(CHUNK):
-                scatter_row(step * CHUNK + t, mixed[:, t * cb : (t + 1) * cb])
+            size = CHUNK // 2
+            moved = [
+                jnp.concatenate(parts[z * size : (z + 1) * size], axis=1) for z in range(2)
+            ]
+            first = [
+                jnp.dot(folded, pair_terms(x), preferred_element_type=F32) for x in moved
+            ]
+            middle = [x + (0.5 * collide_step) * y for x, y in zip(moved, first)]
+            second = [
+                jnp.dot(folded, pair_terms(x), preferred_element_type=F32) for x in middle
+            ]
+            for z in range(2):
+                mixed = moved[z] + collide_step * second[z]
+                for t in range(size):
+                    scatter_row(step * CHUNK + z * size + t, mixed[:, t * cb : (t + 1) * cb])
 
         @pl.loop(0, owners)
         def _(o):
@@ -490,7 +498,7 @@
         flat[pl.ds(0, pad)] = jnp.zeros((pad, LANES), F32)
         flat[pl.ds(pad + owners * 32, pad)] = jnp.zeros((pad, LANES), F32)
 
-        @pl.loop(0, owners // 8)
+        @pl.loop(0, owners // 8, unroll=2)
         def _(b):
             at = pl.ds(pl.multiple_of(pad + b * 256, 128), 256)
             flat[at] = rows_in[pl.ds(b * 8, 8)].astype(F32).reshape(256, LANES)
@@ -498,7 +506,7 @@
         fetch.wait()
         sub = lax.broadcasted_iota(jnp.int32, (8, LANES), 0)
 
-        @pl.loop(0, owners // 8)
+        @pl.loop(0, owners // 8, unroll=2)
         def _(b):
             def take(shift, line):
                 return flat[pl.ds(pad + (b * 8 + shift) * 32 + line, 8, stride=32), :]
@@ -546,8 +554,8 @@
 
         span = SOURCES * SLOTS
         level = lax.broadcasted_iota(jnp.int32, (sections, span), 0).astype(F32)
-        index_a = lax.broadcasted_iota(jnp.int32, (ca, span), 0).astype(F32)
-        index_b = lax.broadcasted_iota(jnp.int32, (cb, span), 0).astype(F32)
+        index_a = lax.broadcasted_iota(jnp.int32, (ca, span), 0).astype(F32).astype(BF16)
+        index_b = lax.broadcasted_iota(jnp.int32, (cb, span), 0).astype(F32).astype(BF16)
 
         def build(step, left, right):
             strength, center, inverse, along, across = (
@@ -559,8 +567,8 @@
             scaled = (level - center) * inverse
             weights = 1.0 / (1.0 + scaled * scaled)
             mass[...] = weights * (strength / jnp.sum(weights, axis=0, keepdims=True))
-            mask = (along == index_a).astype(BF16)
-            right[...] = (across == index_b).astype(BF16)
+            mask = jnp.where(along.astype(BF16) == index_a, jnp.ones((),BF16), jnp.zeros((),BF16))
+            right[...] = jnp.where(across.astype(BF16) == index_b, jnp.ones((),BF16), jnp.zeros((),BF16))
             for k in range(sections):
                 left[k * ca : (k + 1) * ca] = (
                     jnp.broadcast_to(mass[k : k + 1], (ca, span)).astype(BF16) * mask

time: 16.1 us -> 15 us (0.932)
  the two profiles are of different devices: /device:TPU:6 before, /device:TPU:5 now
where the time goes in v3:
time: 15 us; the launch traced here: 14.9 us
  Pallas kernels  14.9 us (99%)
    pallas_call x1, Pallas kernels, body(): pl.pallas_call(functools.partial(kernel, n_slab, n_plane, sections, ca, c...  10.4 us
    pallas_call x1, Pallas kernels, body(): pl.pallas_call(functools.partial(finish, n_plane, owners, sections, ca, c...  4.45 us

profile of v3, /device:TPU:5, one launch (start us, length us, event | category | flops | bytes accessed | tf_op | source)
XLA Modules:
  0.0 14.9 jit_solution(17133069006924659209)
XLA Ops:
  0.0 10.4 %shard_map.82 = (f32[2304,128]{1,0:T(8,128)S(1)}, bf16[16,32,128]{2,1,0:T(8,128)(2,1)S(1)}) custom-call(f32[2048,128]{1,0:T(8,128)} %bitcast.10, f32[32]{0:T(128)} %evap_hbm.1, bf16[32,1024]{1,0:T(8,128)(2,1)} %coal_hbm.1, bf16[1024,640]{1,0:T(8,128)(2,1)} %constant.2.clone.fold_hbm, s32[1,2048]{1,0:T(1,128)} %owner_hbm.1, s32[1,2048]{1,0:T(1,128)} %cell_hbm.1, ...), custom_call_target="tpu_custom_call" | custom-call | tf_op jit(solution)/shard_map/pallas_call | solution.py:623
  10.4 4.5 %shard_map.83 = f32[2048,128]{1,0:T(8,128)} custom-call(f32[2304,128]{1,0:T(8,128)S(1)} %get-tuple-element.7.held, bf16[16,32,128]{2,1,0:T(8,128)(2,1)S(1)} %get-tuple-element.8.rows_in, f32[8]{0:T(128)} %width_hbm.1), custom_call_target="tpu_custom_call" | custom-call | tf_op jit(solution)/shard_map/pallas_call | solution.py:663

commit v4 on v3

--- a/solution.py
+++ b/solution.py
@@ -15,6 +15,7 @@
 SLOTS = 256
 CHUNK = 8
 PAD = 8
+LINES = 24
 SOURCES = 4
 PIECES = 2
 VMEM_BYTES = 56 * 1024 * 1024
@@ -58,10 +59,10 @@
 def kernel(
     n_slab, n_plane, sections, ca, cb, exit_rows,
     fields_hbm, evap_hbm, coal_hbm, fold_hbm, owner_hbm, cell_hbm, pid_hbm,
-    obuf, recv_buf,
-    fbuf, tbuf, edge_in, hbuf, fold, cols_out, cols_in, par, send_buf,
+    obuf, recv_buf, side_in,
+    fbuf, tbuf, edge_in, upright_buf, fold, cols_out, cols_near, cols_in, par, send_buf,
     evap_ref, coal_ref, owner_ref, cell_ref, pid_ref, picks, in_slot,
-    in_sem, arg_sem, halo_send, halo_recv, row_send, row_recv,
+    in_sem, arg_sem, halo_send, halo_recv, row_send, row_recv, side_out, side_send, side_recv,
 ):
     owners = n_slab * n_plane
     rows = sections * ca
@@ -69,6 +70,15 @@
     s = lax.axis_index("slab")
     p = lax.axis_index("plane")
     me = s * n_plane + p
+    barrier = pltpu.get_barrier_semaphore()
+
+    @pl.when(g == 1)
+    def _():
+        for i in range(n_slab):
+            row = jnp.where(2 * s < n_slab, n_slab - 1 - i, i)
+            for j in range(n_plane):
+                pl.semaphore_signal(barrier, inc=1, device_id=(0, row, j), device_id_type=MESH)
+
 
     fpad = fbuf.reshape(sections, 2 * ca + PAD, LANES).at[:, pl.ds(0, 2 * ca), :]
     opad = obuf.reshape(sections, 2 * ca + PAD, LANES).at[:, pl.ds(0, 2 * ca), :]
@@ -99,7 +109,6 @@
         for copy in spray_args:
             copy.start()
 
-    barrier = pltpu.get_barrier_semaphore()
     sides = [
         (s > 0, (g, s - 1, p)),
         (s < n_slab - 1, (g, s + 1, p)),
@@ -113,14 +122,6 @@
         @pl.when(there)
         def _():
             pl.semaphore_signal(barrier, inc=1, device_id=target, device_id_type=MESH)
-
-    @pl.when(g == 1)
-    def _():
-        @pl.loop(0, owners)
-        def _(o):
-            pl.semaphore_signal(
-                barrier, inc=1, device_id=(0, o // n_plane, o % n_plane), device_id_type=MESH
-            )
 
     load.wait()
 
@@ -162,9 +163,16 @@
             tbuf[a + 1] = gather_row(fbuf, a)
 
         lane = lax.broadcasted_iota(jnp.int32, (8, LANES), 1)
-        for h, at in ((0, 0), (1, LANES - 1)):
-            select = (lane == at).astype(BF16)
-            cols_out[h] = dot_last(select, half(fpad, h).astype(BF16))[0:1]
+        line = lax.broadcasted_iota(jnp.int32, (8, LANES), 0)
+        for h, (outer, inner) in enumerate(((0, 1), (LANES - 1, LANES - 2))):
+            select = jnp.logical_or(
+                jnp.logical_and(line == 0, lane == outer), jnp.logical_and(line == 1, lane == inner)
+            ).astype(BF16)
+            columns = dot_last(select, half(fpad, h).astype(BF16))
+            for x in range(rows // LANES):
+                at = slice(x * LANES, (x + 1) * LANES)
+                cols_out[h, x : x + 1] = columns[0:1, at]
+                cols_near[h, x : x + 1] = columns[1:2, at]
 
     def fill_rows():
         @pl.loop(1, ca - 1)
@@ -191,7 +199,11 @@
     def placed_columns():
         sub = lax.broadcasted_iota(jnp.int32, (16, cb), 0)
         lanes = lax.broadcasted_iota(jnp.int32, (16, cb), 1)
-        stack = jnp.concatenate([cols_in[0], cols_in[1], jnp.zeros((14, rows), F32)], axis=0)
+        lined = [
+            jnp.concatenate([cols_in[h, x : x + 1] for x in range(rows // LANES)], axis=1)
+            for h in range(2)
+        ]
+        stack = jnp.concatenate(lined + [jnp.zeros((14, rows), F32)], axis=0)
         place = jnp.logical_or(
             jnp.logical_and(sub == 0, lanes == 0), jnp.logical_and(sub == 1, lanes == cb - 1)
         ).astype(BF16)
@@ -200,20 +212,12 @@
     col_lane = lax.broadcasted_iota(jnp.int32, (sections, cb), 1)
     col_row = lax.broadcasted_iota(jnp.int32, (sections, cb), 0)
 
-    def column_halo(a):
-        return jnp.concatenate(
-            [hbuf[h, pl.ds(a, sections, stride=ca + PAD), :] for h in range(2)], axis=1
-        )
-
-    def neighbours(a, with_columns):
+    def neighbours(a):
         c = tbuf[a + 1]
         up = tbuf[a]
         left = jnp.where(col_lane == 0, 0.0, pltpu.roll(c, 1, 1))
         right = jnp.where(col_lane == cb - 1, 0.0, pltpu.roll(c, cb - 1, 1))
-        beside = left + right
-        if with_columns:
-            beside += column_halo(a)
-        lap = up + tbuf[a + 2] + beside - 4.0 * c
+        lap = up + tbuf[a + 2] + (left + right) - 4.0 * c
         return c, up, lap
 
     def scatter_row(a, value):
@@ -240,12 +244,20 @@
         cell = cell_ref[...]
         across = jnp.bitwise_and(cell, cb - 1)
         along = jnp.right_shift(cell, cb.bit_length() - 1)
-        par[4:5] = (pid_ref[...] * ca + along).astype(F32)
+        par[3:4] = pid_ref[...].astype(F32)
+        par[4:5] = along.astype(F32)
         par[5:6] = across.astype(F32)
+        half_cb = cb // 2
+        last_line = ca // 2 - 1
         number = lax.broadcasted_iota(jnp.int32, (1, exit_rows), 1)
-        half_cb = cb // 2
-        par[6:7] = jnp.bitwise_and(number, half_cb - 1).astype(F32)
-        par[7:8] = (jnp.right_shift(number, half_cb.bit_length() - 1) + 1).astype(F32)
+        spot = jnp.bitwise_and(number, half_cb - 1)
+        line = jnp.right_shift(number, half_cb.bit_length() - 1)
+        beside = half_cb + 1 + line
+        place = jnp.where(spot == half_cb - 1, -beside, half_cb + ca)
+        place = jnp.where(spot == 0, beside, place)
+        place = jnp.where(line == last_line, -1 - spot, place)
+        par[6:7] = jnp.where(line == 0, 1 + spot, place).astype(F32)
+        par[7:8] = jnp.zeros((1, exit_rows), F32)
         places = lax.broadcasted_iota(jnp.int32, (SLOTS, exit_rows), 0).astype(F32)
         in_slot[...] = (slot == places).astype(BF16)
         group = 16
@@ -310,25 +322,24 @@
             jnp.concatenate([hi, mid, low], axis=0), halve, preferred_element_type=F32
         )
         coarse = sums[:count] + sums[count : 2 * count] + sums[2 * count :]
-        for v in range(2):
-            for k, part in enumerate(split_hi_lo(coarse[v * ca : (v + 1) * ca])):
-                part = part.astype(F32)
-                for i in range(ca // 2):
-                    par[2 * v + k : 2 * v + k + 1, i * (cb // 2) : (i + 1) * (cb // 2)] = part[
-                        2 * i : 2 * i + 1
-                    ]
+        flux_part = coarse[:ca].astype(BF16).astype(F32)
+        skew_hi, skew_lo = split_hi_lo(coarse[ca : 2 * ca])
+        for k, part in enumerate((flux_part, skew_hi.astype(F32), skew_lo.astype(F32))):
+            for i in range(ca // 2):
+                par[k : k + 1, i * (cb // 2) : (i + 1) * (cb // 2)] = part[2 * i : 2 * i + 1]
         side_hi, side_lo = split_hi_lo(0.25 * paired[2 * ca :])
         lane = lax.broadcasted_iota(jnp.int32, (8, cb), 1)
         line = lax.broadcasted_iota(jnp.int32, (8, cb), 0)
         ends = jnp.logical_or(
             jnp.logical_and(line == 0, lane == 0), jnp.logical_and(line == 1, lane == cb - 1)
         ).astype(BF16)
-        side = dot_last(ends, jnp.concatenate([side_hi, side_lo], axis=0))
-        edge_hi, edge_lo = split_hi_lo(coarse[2 * ca :])
-        edge_hi, edge_lo = edge_hi.astype(F32), edge_lo.astype(F32)
-        edges = jnp.concatenate(
-            [x[n : n + 1] for n in range(4) for x in (edge_hi, edge_lo)] + [side], axis=0
-        ).astype(BF16)
+        side = dot_last(ends, side_hi) + dot_last(ends, side_lo)
+        edge = coarse[2 * ca :]
+        side_out[0] = jnp.concatenate([side[0:1], side[1:2]], axis=1)
+        side_out[1] = edge[1:2]
+        side_out[2] = edge[3:4]
+        blank = jnp.zeros((7, LANES), F32)
+        edges = [jnp.concatenate([blank, edge[2 * x : 2 * x + 1]], axis=0) for x in range(2)]
 
         values = par[...].astype(BF16)
         tiled = jnp.concatenate([values] * group, axis=0)
@@ -338,27 +349,35 @@
             picked = tiled * picks[pl.ds(pl.multiple_of(b * group * 8, group * 8), group * 8)]
             packed = dot_last(picked, in_slot[...]).reshape(group, 8, SLOTS)
             send_buf[pl.ds(b * group, group)] = jnp.concatenate(
-                [
-                    packed[:, :, :LANES].astype(BF16),
-                    packed[:, :, LANES:].astype(BF16),
-                    jnp.broadcast_to(edges[None], (group, 16, LANES)),
-                ],
+                [packed[:, :, :LANES] + edges[0][None], packed[:, :, LANES:] + edges[1][None]],
                 axis=1,
-            )
+            ).astype(BF16)
 
         pl.semaphore_wait(barrier, near + owners)
 
-        @pl.loop(0, owners)
-        def _(k):
-            o = jnp.where(2 * s < n_slab, owners - 1 - k, k)
-            pltpu.make_async_remote_copy(
-                src_ref=send_buf.at[o],
-                dst_ref=recv_buf.at[me],
-                send_sem=row_send.at[o],
-                recv_sem=row_recv.at[me],
-                device_id=(1, o // n_plane, o % n_plane),
-                device_id_type=MESH,
-            ).start()
+        for i in range(n_slab):
+            row = jnp.where(2 * s < n_slab, n_slab - 1 - i, i)
+            for j in range(n_plane):
+                pltpu.make_async_remote_copy(
+                    src_ref=side_out,
+                    dst_ref=side_in.at[me],
+                    send_sem=side_send.at[row * n_plane + j],
+                    recv_sem=side_recv.at[me],
+                    device_id=(1, row, j),
+                    device_id_type=MESH,
+                ).start()
+
+        for i in range(n_slab):
+            row = jnp.where(2 * s < n_slab, n_slab - 1 - i, i)
+            for j in range(n_plane):
+                pltpu.make_async_remote_copy(
+                    src_ref=send_buf.at[row * n_plane + j],
+                    dst_ref=recv_buf.at[me],
+                    send_sem=row_send.at[row * n_plane + j],
+                    recv_sem=row_recv.at[me],
+                    device_id=(1, row, j),
+                    device_id_type=MESH,
+                ).start()
 
         extract_columns()
         start_halo((0, 1, 2, 3))
@@ -370,7 +389,7 @@
         def _(step):
             for t in range(CHUNK):
                 a = step * CHUNK + t
-                c, _, lap = neighbours(a, False)
+                c, _, lap = neighbours(a)
                 back = jnp.where(jnp.bitwise_and(col_row, layers - 1) == 0, 0.0, pltpu.roll(c, 1, 0))
                 du = c - back
                 d, m, q, e = (c[v * layers : (v + 1) * layers] for v in range(4))
@@ -408,6 +427,15 @@
                 device_id_type=MESH,
             ).wait_send()
 
+            pltpu.make_async_remote_copy(
+                src_ref=side_out,
+                dst_ref=side_in.at[me],
+                send_sem=side_send.at[o],
+                recv_sem=side_recv.at[me],
+                device_id=(1, o // n_plane, o % n_plane),
+                device_id_type=MESH,
+            ).wait_send()
+
     @pl.when(g == 1)
     def _():
         extract_columns()
@@ -421,41 +449,78 @@
         for k in range(sections):
             evap = jnp.where(col_row == k, evap_ref[k], evap)
         speeds = 0.2 + 0.5 * col_row.astype(F32) / (sections - 1)
+        for a in (0, ca + 1):
+            tbuf[a] = jnp.zeros((sections, cb), F32)
+
+        def moved_from(c, up, lap):
+            width = c.shape[1]
+            lost = evap[:, :width] * c
+            gained = jnp.where(
+                col_row[:, :width] == sections - 1, 0.0, pltpu.roll(lost, sections - 1, 0)
+            )
+            return c - speeds[:, :width] * (c - up) + diffusion * lap - lost + gained
+
+        def collide(moved):
+            first = [jnp.dot(folded, pair_terms(x), preferred_element_type=F32) for x in moved]
+            middle = [x + (0.5 * collide_step) * y for x, y in zip(moved, first)]
+            second = [jnp.dot(folded, pair_terms(x), preferred_element_type=F32) for x in middle]
+            return [x + collide_step * y for x, y in zip(moved, second)]
+
+        @pl.loop(0, ca // CHUNK)
+        def _(step):
+            size = CHUNK // 2
+            moved = [
+                jnp.concatenate(
+                    [moved_from(*neighbours(step * CHUNK + z * size + t)) for t in range(size)],
+                    axis=1,
+                )
+                for z in range(2)
+            ]
+            for z, mixed in enumerate(collide(moved)):
+                for t in range(size):
+                    scatter_row(step * CHUNK + z * size + t, mixed[:, t * cb : (t + 1) * cb])
 
         wait_halo()
         for side, a in enumerate((0, ca + 1)):
             tbuf[a] = edge_in[side]
-        placed = placed_columns()
-        for h in range(2):
-            hbuf.reshape(2, sections, ca + PAD, LANES)[h, :, pl.ds(0, ca), :] = placed[
-                :, h * LANES : (h + 1) * LANES
-            ].reshape(sections, ca, LANES)
-
-        @pl.loop(0, ca // CHUNK)
-        def _(step):
-            parts = []
-            for t in range(CHUNK):
-                c, up, lap = neighbours(step * CHUNK + t, True)
-                lost = evap * c
-                gained = jnp.where(
-                    col_row == sections - 1, 0.0, pltpu.roll(lost, sections - 1, 0)
+        tile_lane = lax.broadcasted_iota(jnp.int32, (8, LANES), 1)
+        wide_lane = lax.broadcasted_iota(jnp.int32, (sections, LANES), 1)
+
+        def upright(x, pair):
+            folds = LANES // ca
+            for k in range(folds):
+                turned = [
+                    pltpu.roll(pair[h], (LANES + (h - k) * ca) % LANES, 1) for h in range(2)
+                ]
+                upright_buf[x, pl.ds(k, sections // folds, stride=folds), :] = jnp.where(
+                    tile_lane < ca, turned[0], turned[1]
                 )
-                parts.append(c - speeds * (c - up) + diffusion * lap - lost + gained)
-            size = CHUNK // 2
-            moved = [
-                jnp.concatenate(parts[z * size : (z + 1) * size], axis=1) for z in range(2)
-            ]
-            first = [
-                jnp.dot(folded, pair_terms(x), preferred_element_type=F32) for x in moved
-            ]
-            middle = [x + (0.5 * collide_step) * y for x, y in zip(moved, first)]
-            second = [
-                jnp.dot(folded, pair_terms(x), preferred_element_type=F32) for x in middle
-            ]
-            for z in range(2):
-                mixed = moved[z] + collide_step * second[z]
-                for t in range(size):
-                    scatter_row(step * CHUNK + z * size + t, mixed[:, t * cb : (t + 1) * cb])
+            return upright_buf[x]
+
+        own = upright(0, (cols_out[0], cols_out[1]))
+        inner = upright(1, (cols_near[0], cols_near[1]))
+        outer = upright(2, (cols_in[0], cols_in[1]))
+        above = pltpu.roll(own, 1, 1)
+        below = pltpu.roll(own, LANES - 1, 1)
+        parts = []
+        for a in (0, ca - 1):
+            c, up, lap = neighbours(a)
+            lap += jnp.where(col_lane == 0, outer[:, a : a + 1], 0.0)
+            lap += jnp.where(col_lane == cb - 1, outer[:, ca + a : ca + a + 1], 0.0)
+            parts.append(moved_from(c, up, lap))
+        parts.append(moved_from(own, above, above + below + inner + outer - 4.0 * own))
+        (mixed,) = collide([jnp.concatenate(parts, axis=1)])
+        columns = mixed[:, 2 * cb :]
+        for a in range(1, ca - 1):
+            for h, target in enumerate((0, LANES - 1)):
+                at = lines(a, h)
+                obuf[at, :] = jnp.where(
+                    wide_lane == target,
+                    pltpu.roll(columns, (LANES + target - h * ca - a) % LANES, 1),
+                    obuf[at, :],
+                )
+        for x, a in enumerate((0, ca - 1)):
+            scatter_row(a, mixed[:, x * cb : (x + 1) * cb])
 
         @pl.loop(0, owners)
         def _(o):
@@ -468,10 +533,19 @@
                 device_id_type=MESH,
             ).wait_recv()
 
+            pltpu.make_async_remote_copy(
+                src_ref=side_out,
+                dst_ref=side_in.at[o],
+                send_sem=side_send.at[o],
+                recv_sem=side_recv.at[o],
+                device_id=(0, s, p),
+                device_id_type=MESH,
+            ).wait_recv()
+
 
 def finish(
     n_plane, owners, sections, ca, cb,
-    held, rows_in, width_hbm,
+    held, rows_in, sides_in, width_hbm,
     out_hbm,
     obuf, flat, par, mass, left_even, left_odd, right_even, right_odd, width_ref, arg_sem, out_sem,
 ):
@@ -493,15 +567,18 @@
         fetch.start()
         fill = pltpu.make_async_copy(whole, obuf, out_sem.at[PIECES])
         fill.start()
-        pad = n_plane * 32
         half_cb = cb // 2
+        pad = n_plane * LINES
         flat[pl.ds(0, pad)] = jnp.zeros((pad, LANES), F32)
-        flat[pl.ds(pad + owners * 32, pad)] = jnp.zeros((pad, LANES), F32)
+        flat[pl.ds(pad + owners * LINES, pad)] = jnp.zeros((pad, LANES), F32)
 
         @pl.loop(0, owners // 8, unroll=2)
         def _(b):
-            at = pl.ds(pl.multiple_of(pad + b * 256, 128), 256)
-            flat[at] = rows_in[pl.ds(b * 8, 8)].astype(F32).reshape(256, LANES)
+            for o in range(8):
+                at = pl.multiple_of(pad + (b * 8 + o) * LINES, 8)
+                flat[pl.ds(at, 16)] = rows_in[b * 8 + o].astype(F32)
+                for x in range(3):
+                    flat[pl.ds(at + 16 + x, 1)] = sides_in[b * 8 + o, x]
 
         fetch.wait()
         sub = lax.broadcasted_iota(jnp.int32, (8, LANES), 0)
@@ -509,44 +586,52 @@
         @pl.loop(0, owners // 8, unroll=2)
         def _(b):
             def take(shift, line):
-                return flat[pl.ds(pad + (b * 8 + shift) * 32 + line, 8, stride=32), :]
+                return flat[pl.ds(pad + (b * 8 + shift) * LINES + line, 8, stride=LINES), :]
 
             plane_at = lax.rem(b * 8 + sub, n_plane)
-            first_plane = plane_at == 0
-            last_plane = plane_at == n_plane - 1
-            above = [take(-n_plane, 16 + 4 + x) for x in range(4)]
-            below = [take(n_plane, 16 + x) for x in range(4)]
-            before = jnp.where(first_plane, 0.0, take(-1, 16 + 9))
-            behind = jnp.where(last_plane, 0.0, take(1, 16 + 8))
+            above = take(-n_plane, 15), take(-n_plane, 18)
+            below = take(n_plane, 7), take(n_plane, 17)
+            before = jnp.where(plane_at == 0, 0.0, take(-1, 16))
+            behind = jnp.where(plane_at == n_plane - 1, 0.0, take(1, 16))
 
             def pick(table, index):
                 return jnp.take_along_axis(table, index, axis=1, mode="promise_in_bounds")
 
             for h in range(2):
-                got = [take(0, h * 8 + x) for x in range(8)]
-                spot = got[6].astype(jnp.int32)
-                line = got[7].astype(jnp.int32)
-                slot_line = 2 * jnp.maximum(line - 1, 0)
-                flux = got[0] + got[1]
-                skew = got[2] + got[3]
-                for tables, here in ((above, line == 1), (below, line == ca // 2)):
-                    f0, f1, u0, u1 = (pick(table, spot) for table in tables)
-                    flux += jnp.where(here, f0 + f1, 0.0)
-                    skew += jnp.where(here, u0 + u1, 0.0)
-                for table, here in ((before, spot == 0), (behind, spot == half_cb - 1)):
-                    f0, u0, f1, u1 = (pick(table, slot_line + ca * x) for x in range(4))
-                    flux += jnp.where(here, f0 + f1, 0.0)
-                    skew += jnp.where(here, u0 + u1, 0.0)
-                code = got[4].astype(jnp.int32)
-                plume = jnp.right_shift(code, ca.bit_length() - 1)
+                got = [take(0, h * 8 + x) for x in range(7)]
+                place = got[6].astype(jnp.int32)
+                size = jnp.abs(place)
+                on_row = size <= half_cb
+                spot = jnp.clip(size - 1, 0, half_cb - 1)
+                line = jnp.clip(size - half_cb - 1, 0, ca // 2 - 1)
+                line = jnp.where(on_row, jnp.where(place < 0, ca // 2 - 1, 0), line)
+                inside = size == half_cb + ca
+                in_column = jnp.logical_not(jnp.logical_or(on_row, inside))
+                first_row = jnp.logical_and(on_row, place > 0)
+                last_row = jnp.logical_and(on_row, place < 0)
+                first_column = jnp.logical_or(size == 1, jnp.logical_and(in_column, place > 0))
+                last_column = jnp.logical_or(
+                    size == half_cb, jnp.logical_and(in_column, place < 0)
+                )
+                flux = got[0]
+                skew = got[1] + got[2]
+                for tables, here in ((above, first_row), (below, last_row)):
+                    flux += jnp.where(here, pick(tables[0], spot), 0.0)
+                    skew += jnp.where(here, pick(tables[1], spot), 0.0)
+                for table, base, here in (
+                    (before, 2 * ca, first_column),
+                    (behind, 0, last_column),
+                ):
+                    flux += jnp.where(here, pick(table, 2 * line + base), 0.0)
+                    skew += jnp.where(here, pick(table, 2 * line + base + ca), 0.0)
                 spread = jnp.full((8, LANES), width_ref[0], F32)
                 for k in range(1, plumes):
-                    spread = jnp.where(plume == k, width_ref[k], spread)
+                    spread = jnp.where(got[3] == float(k), width_ref[k], spread)
                 values = (
-                    jnp.where(line > 0, jnp.sqrt(1.0 + flux * flux), 0.0),
+                    jnp.where(place != 0, jnp.sqrt(1.0 + flux * flux), 0.0),
                     (sections - 1) * jax.nn.sigmoid(skew),
                     1.0 / spread,
-                    jnp.bitwise_and(code, ca - 1).astype(F32),
+                    got[4],
                     got[5],
                 )
                 for x, value in enumerate(values):
@@ -620,24 +705,26 @@
     kept = fold.shape[1]
     hbm = pl.BlockSpec(memory_space=pl.ANY)
     vmem = pl.BlockSpec(memory_space=pltpu.VMEM)
-    held, rows_in = pl.pallas_call(
+    held, rows_in, sides_in = pl.pallas_call(
         functools.partial(kernel, n_slab, n_plane, sections, ca, cb, exit_rows),
         out_shape=[
             pltpu.VMEM((2 * rows + sections * PAD, LANES), F32),
-            pltpu.VMEM((owners, 32, LANES), BF16),
+            pltpu.VMEM((owners, 16, LANES), BF16),
+            pltpu.VMEM((owners, 3, 1, LANES), F32),
         ],
         in_specs=[hbm] * 7,
-        out_specs=[vmem] * 2,
+        out_specs=[vmem] * 3,
         scratch_shapes=[
             pltpu.VMEM((2 * rows + sections * PAD, LANES), F32),
             pltpu.VMEM((ca + 2, sections, cb), F32),
             pltpu.VMEM((2, sections, cb), F32),
-            pltpu.VMEM((2, rows + sections * PAD, LANES), F32),
+            pltpu.VMEM((3, sections, LANES), F32),
             pltpu.VMEM((sections * sections, kept), BF16),
-            pltpu.VMEM((2, 1, rows), F32),
-            pltpu.VMEM((2, 1, rows), F32),
+            pltpu.VMEM((2, rows // LANES, LANES), F32),
+            pltpu.VMEM((2, rows // LANES, LANES), F32),
+            pltpu.VMEM((2, rows // LANES, LANES), F32),
             pltpu.VMEM((8, exit_rows), F32),
-            pltpu.VMEM((owners, 32, LANES), BF16),
+            pltpu.VMEM((owners, 16, LANES), BF16),
             pltpu.SMEM(evap_rates.shape, F32),
             pltpu.VMEM(coal_kernel.shape, BF16),
             pltpu.VMEM((1, exit_rows), jnp.int32),
@@ -649,6 +736,9 @@
             pltpu.SemaphoreType.DMA((4,)),
             pltpu.SemaphoreType.DMA((4,)),
             pltpu.SemaphoreType.DMA((4,)),
+            pltpu.SemaphoreType.DMA((owners,)),
+            pltpu.SemaphoreType.DMA((owners,)),
+            pltpu.VMEM((3, 1, LANES), F32),
             pltpu.SemaphoreType.DMA((owners,)),
             pltpu.SemaphoreType.DMA((owners,)),
         ],
@@ -663,11 +753,11 @@
     out = pl.pallas_call(
         functools.partial(finish, n_plane, owners, sections, ca, cb),
         out_shape=jax.ShapeDtypeStruct((2 * rows, LANES), F32),
-        in_specs=[vmem, vmem, hbm],
+        in_specs=[vmem, vmem, vmem, hbm],
         out_specs=hbm,
         scratch_shapes=[
             pltpu.VMEM((sections, 2 * ca, LANES), F32),
-            pltpu.VMEM(((owners + 2 * n_plane) * 32, LANES), F32),
+            pltpu.VMEM(((owners + 2 * n_plane) * LINES, LANES), F32),
             pltpu.VMEM((5, owners, SLOTS), F32),
             pltpu.VMEM((sections, span), F32),
             pltpu.VMEM((rows, span), BF16),
@@ -682,6 +772,7 @@
     )(
         pltpu.with_memory_space_constraint(held, pltpu.VMEM),
         pltpu.with_memory_space_constraint(rows_in, pltpu.VMEM),
+        pltpu.with_memory_space_constraint(sides_in, pltpu.VMEM),
         plume_width,
     )
     out = out.reshape(rows // 8, 2, 8, LANES).transpose(0, 2, 1, 3)

time: 15 us -> 14.5 us (0.967)
  Pallas kernels: 14.9 us -> 14.3 us
    pallas_call x1, Pallas kernels: 10.4 us -> 9.93 us  [body(): pl.pallas_call(functools.partial(kernel, n_slab, n_plane, sections, ca, c...]
where the time goes in v4:
time: 14.5 us; the launch traced here: 14.3 us
  Pallas kernels  14.3 us (99%)
    pallas_call x1, Pallas kernels, body(): pl.pallas_call(functools.partial(kernel, n_slab, n_plane, sections, ca, c...  9.93 us
    pallas_call x1, Pallas kernels, body(): pl.pallas_call(functools.partial(finish, n_plane, owners, sections, ca, c...  4.37 us

profile of v4, /device:TPU:5, one launch (start us, length us, event | category | flops | bytes accessed | tf_op | source)
XLA Modules:
  0.0 14.3 jit_solution(15798229907845292236)
XLA Ops:
  0.0 9.9 %shard_map.82 = (f32[2304,128]{1,0:T(8,128)S(1)}, bf16[16,16,128]{2,1,0:T(8,128)(2,1)S(1)}, f32[16,3,1,128]{3,2,1,0:T(1,128)S(1)}) custom-call(f32[2048,128]{1,0:T(8,128)} %bitcast.10, f32[32]{0:T(128)} %evap_hbm.1, bf16[32,1024]{1,0:T(8,128)(2,1)} %coal_hbm.1, bf16[1024,640]{1,0:T(8,128)(2,1)} %constant.2.clone.fold_hbm, s32[1,2048]{1,0:T(1,128)} %owner_hbm.1, ...), custom_call_target="tpu_custom_call" | custom-call | tf_op jit(solution)/shard_map/pallas_call | solution.py:708
  9.9 4.4 %shard_map.83 = f32[2048,128]{1,0:T(8,128)} custom-call(f32[2304,128]{1,0:T(8,128)S(1)} %get-tuple-element.8.held, bf16[16,16,128]{2,1,0:T(8,128)(2,1)S(1)} %get-tuple-element.9.rows_in, f32[16,3,1,128]{3,2,1,0:T(1,128)S(1)} %get-tuple-element.10.sides_in, f32[8]{0:T(128)} %width_hbm.1), custom_call_target="tpu_custom_call" | custom-call | tf_op jit(solution)/shard_map/pallas_call | solution.py:753

commit v5 on v4

--- a/solution.py
+++ b/solution.py
@@ -59,10 +59,10 @@
 def kernel(
     n_slab, n_plane, sections, ca, cb, exit_rows,
     fields_hbm, evap_hbm, coal_hbm, fold_hbm, owner_hbm, cell_hbm, pid_hbm,
-    obuf, recv_buf, side_in,
+    obuf, recv_buf,
     fbuf, tbuf, edge_in, upright_buf, fold, cols_out, cols_near, cols_in, par, send_buf,
     evap_ref, coal_ref, owner_ref, cell_ref, pid_ref, picks, in_slot,
-    in_sem, arg_sem, halo_send, halo_recv, row_send, row_recv, side_out, side_send, side_recv,
+    in_sem, arg_sem, halo_send, halo_recv, row_send, row_recv,
 ):
     owners = n_slab * n_plane
     rows = sections * ca
@@ -335,9 +335,15 @@
         ).astype(BF16)
         side = dot_last(ends, side_hi) + dot_last(ends, side_lo)
         edge = coarse[2 * ca :]
-        side_out[0] = jnp.concatenate([side[0:1], side[1:2]], axis=1)
-        side_out[1] = edge[1:2]
-        side_out[2] = edge[3:4]
+        more = jnp.concatenate(
+            [
+                jnp.concatenate([side[0:1], side[1:2]], axis=1),
+                edge[1:2],
+                edge[3:4],
+                jnp.zeros((5, LANES), F32),
+            ],
+            axis=0,
+        )
         blank = jnp.zeros((7, LANES), F32)
         edges = [jnp.concatenate([blank, edge[2 * x : 2 * x + 1]], axis=0) for x in range(2)]
 
@@ -349,23 +355,15 @@
             picked = tiled * picks[pl.ds(pl.multiple_of(b * group * 8, group * 8), group * 8)]
             packed = dot_last(picked, in_slot[...]).reshape(group, 8, SLOTS)
             send_buf[pl.ds(b * group, group)] = jnp.concatenate(
-                [packed[:, :, :LANES] + edges[0][None], packed[:, :, LANES:] + edges[1][None]],
+                [
+                    packed[:, :, :LANES] + edges[0][None],
+                    packed[:, :, LANES:] + edges[1][None],
+                    jnp.broadcast_to(more[None], (group, 8, LANES)),
+                ],
                 axis=1,
             ).astype(BF16)
 
         pl.semaphore_wait(barrier, near + owners)
-
-        for i in range(n_slab):
-            row = jnp.where(2 * s < n_slab, n_slab - 1 - i, i)
-            for j in range(n_plane):
-                pltpu.make_async_remote_copy(
-                    src_ref=side_out,
-                    dst_ref=side_in.at[me],
-                    send_sem=side_send.at[row * n_plane + j],
-                    recv_sem=side_recv.at[me],
-                    device_id=(1, row, j),
-                    device_id_type=MESH,
-                ).start()
 
         for i in range(n_slab):
             row = jnp.where(2 * s < n_slab, n_slab - 1 - i, i)
@@ -423,15 +421,6 @@
                 dst_ref=recv_buf.at[me],
                 send_sem=row_send.at[o],
                 recv_sem=row_recv.at[me],
-                device_id=(1, o // n_plane, o % n_plane),
-                device_id_type=MESH,
-            ).wait_send()
-
-            pltpu.make_async_remote_copy(
-                src_ref=side_out,
-                dst_ref=side_in.at[me],
-                send_sem=side_send.at[o],
-                recv_sem=side_recv.at[me],
                 device_id=(1, o // n_plane, o % n_plane),
                 device_id_type=MESH,
             ).wait_send()
@@ -533,19 +522,10 @@
                 device_id_type=MESH,
             ).wait_recv()
 
-            pltpu.make_async_remote_copy(
-                src_ref=side_out,
-                dst_ref=side_in.at[o],
-                send_sem=side_send.at[o],
-                recv_sem=side_recv.at[o],
-                device_id=(0, s, p),
-                device_id_type=MESH,
-            ).wait_recv()
-
 
 def finish(
     n_plane, owners, sections, ca, cb,
-    held, rows_in, sides_in, width_hbm,
+    held, rows_in, width_hbm,
     out_hbm,
     obuf, flat, par, mass, left_even, left_odd, right_even, right_odd, width_ref, arg_sem, out_sem,
 ):
@@ -565,8 +545,6 @@
     def _():
         fetch = pltpu.make_async_copy(width_hbm, width_ref, arg_sem)
         fetch.start()
-        fill = pltpu.make_async_copy(whole, obuf, out_sem.at[PIECES])
-        fill.start()
         half_cb = cb // 2
         pad = n_plane * LINES
         flat[pl.ds(0, pad)] = jnp.zeros((pad, LANES), F32)
@@ -576,9 +554,7 @@
         def _(b):
             for o in range(8):
                 at = pl.multiple_of(pad + (b * 8 + o) * LINES, 8)
-                flat[pl.ds(at, 16)] = rows_in[b * 8 + o].astype(F32)
-                for x in range(3):
-                    flat[pl.ds(at + 16 + x, 1)] = sides_in[b * 8 + o, x]
+                flat[pl.ds(at, LINES)] = rows_in[b * 8 + o].astype(F32)
 
         fetch.wait()
         sub = lax.broadcasted_iota(jnp.int32, (8, LANES), 0)
@@ -659,7 +635,7 @@
                     jnp.broadcast_to(mass[k : k + 1], (ca, span)).astype(BF16) * mask
                 )
 
-        def add(left, right, first, count):
+        def add(left, right, first, count, base):
             added = dot_last(left[first * ca : (first + count) * ca], right[...])
             tiles = jnp.stack(
                 [
@@ -668,25 +644,27 @@
                 ],
                 axis=1,
             )
-            obuf[first : first + count] += tiles.reshape(count, 2 * ca, LANES)
+            obuf[first : first + count] = base[first : first + count] + tiles.reshape(
+                count, 2 * ca, LANES
+            )
 
         build(0, left_even, right_even)
-        fill.wait()
         steps = owners // SOURCES
 
-        @pl.loop(0, steps // 2 - 1)
+        add(left_even, right_even, 0, sections, whole)
+        build(1, left_odd, right_odd)
+
+        @pl.loop(1, steps // 2)
         def _(i):
-            add(left_even, right_even, 0, sections)
+            add(left_odd, right_odd, 0, sections, obuf)
+            build(2 * i, left_even, right_even)
+            add(left_even, right_even, 0, sections, obuf)
             build(2 * i + 1, left_odd, right_odd)
-            add(left_odd, right_odd, 0, sections)
-            build(2 * i + 2, left_even, right_even)
-
-        add(left_even, right_even, 0, sections)
-        build(steps - 1, left_odd, right_odd)
+
         each = sections // PIECES
         stores = []
         for c in range(PIECES):
-            add(left_odd, right_odd, c * each, each)
+            add(left_odd, right_odd, c * each, each, obuf)
             at = pl.ds(c * each, each)
             stores.append(
                 pltpu.make_async_copy(obuf.at[at], out_whole.at[at], out_sem.at[c])
@@ -705,15 +683,14 @@
     kept = fold.shape[1]
     hbm = pl.BlockSpec(memory_space=pl.ANY)
     vmem = pl.BlockSpec(memory_space=pltpu.VMEM)
-    held, rows_in, sides_in = pl.pallas_call(
+    held, rows_in = pl.pallas_call(
         functools.partial(kernel, n_slab, n_plane, sections, ca, cb, exit_rows),
         out_shape=[
             pltpu.VMEM((2 * rows + sections * PAD, LANES), F32),
-            pltpu.VMEM((owners, 16, LANES), BF16),
-            pltpu.VMEM((owners, 3, 1, LANES), F32),
+            pltpu.VMEM((owners, LINES, LANES), BF16),
         ],
         in_specs=[hbm] * 7,
-        out_specs=[vmem] * 3,
+        out_specs=[vmem] * 2,
         scratch_shapes=[
             pltpu.VMEM((2 * rows + sections * PAD, LANES), F32),
             pltpu.VMEM((ca + 2, sections, cb), F32),
@@ -724,7 +701,7 @@
             pltpu.VMEM((2, rows // LANES, LANES), F32),
             pltpu.VMEM((2, rows // LANES, LANES), F32),
             pltpu.VMEM((8, exit_rows), F32),
-            pltpu.VMEM((owners, 16, LANES), BF16),
+            pltpu.VMEM((owners, LINES, LANES), BF16),
             pltpu.SMEM(evap_rates.shape, F32),
             pltpu.VMEM(coal_kernel.shape, BF16),
             pltpu.VMEM((1, exit_rows), jnp.int32),
@@ -736,9 +713,6 @@
             pltpu.SemaphoreType.DMA((4,)),
             pltpu.SemaphoreType.DMA((4,)),
             pltpu.SemaphoreType.DMA((4,)),
-            pltpu.SemaphoreType.DMA((owners,)),
-            pltpu.SemaphoreType.DMA((owners,)),
-            pltpu.VMEM((3, 1, LANES), F32),
             pltpu.SemaphoreType.DMA((owners,)),
             pltpu.SemaphoreType.DMA((owners,)),
         ],
@@ -753,7 +727,7 @@
     out = pl.pallas_call(
         functools.partial(finish, n_plane, owners, sections, ca, cb),
         out_shape=jax.ShapeDtypeStruct((2 * rows, LANES), F32),
-        in_specs=[vmem, vmem, vmem, hbm],
+        in_specs=[vmem, vmem, hbm],
         out_specs=hbm,
         scratch_shapes=[
             pltpu.VMEM((sections, 2 * ca, LANES), F32),
@@ -766,13 +740,12 @@
             pltpu.VMEM((cb, span), BF16),
             pltpu.SMEM(plume_width.shape, F32),
             pltpu.SemaphoreType.DMA,
-            pltpu.SemaphoreType.DMA((PIECES + 1,)),
+            pltpu.SemaphoreType.DMA((PIECES,)),
         ],
         compiler_params=pltpu.CompilerParams(vmem_limit_bytes=VMEM_BYTES),
     )(
         pltpu.with_memory_space_constraint(held, pltpu.VMEM),
         pltpu.with_memory_space_constraint(rows_in, pltpu.VMEM),
-        pltpu.with_memory_space_constraint(sides_in, pltpu.VMEM),
         plume_width,
     )
     out = out.reshape(rows // 8, 2, 8, LANES).transpose(0, 2, 1, 3)

time: 14.5 us -> 14.1 us (0.972)
  Pallas kernels: 14.3 us -> 14 us
    pallas_call x1, Pallas kernels: 9.93 us -> 9.74 us  [body(): pl.pallas_call(functools.partial(kernel, n_slab, n_plane, sections, ca, c...]
where the time goes in v5:
time: 14.1 us; the launch traced here: 14 us
  Pallas kernels  14 us (99%)
    pallas_call x1, Pallas kernels, body(): pl.pallas_call(functools.partial(kernel, n_slab, n_plane, sections, ca, c...  9.74 us
    pallas_call x1, Pallas kernels, body(): pl.pallas_call(functools.partial(finish, n_plane, owners, sections, ca, c...  4.26 us

profile of v5, /device:TPU:5, one launch (start us, length us, event | category | flops | bytes accessed | tf_op | source)
XLA Modules:
  0.0 14.0 jit_solution(2946685753190136609)
XLA Ops:
  0.0 9.7 %shard_map.82 = (f32[2304,128]{1,0:T(8,128)S(1)}, bf16[16,24,128]{2,1,0:T(8,128)(2,1)S(1)}) custom-call(f32[2048,128]{1,0:T(8,128)} %bitcast.10, f32[32]{0:T(128)} %evap_hbm.1, bf16[32,1024]{1,0:T(8,128)(2,1)} %coal_hbm.1, bf16[1024,640]{1,0:T(8,128)(2,1)} %constant.2.clone.fold_hbm, s32[1,2048]{1,0:T(1,128)} %owner_hbm.1, s32[1,2048]{1,0:T(1,128)} %cell_hbm.1, ...), custom_call_target="tpu_custom_call" | custom-call | tf_op jit(solution)/shard_map/pallas_call | solution.py:686
  9.7 4.3 %shard_map.83 = f32[2048,128]{1,0:T(8,128)} custom-call(f32[2304,128]{1,0:T(8,128)S(1)} %get-tuple-element.7.held, bf16[16,24,128]{2,1,0:T(8,128)(2,1)S(1)} %get-tuple-element.8.rows_in, f32[8]{0:T(128)} %width_hbm.1), custom_call_target="tpu_custom_call" | custom-call | tf_op jit(solution)/shard_map/pallas_call | solution.py:727

commit v6 on v4

--- a/solution.py
+++ b/solution.py
@@ -58,10 +58,10 @@
 
 def kernel(
     n_slab, n_plane, sections, ca, cb, exit_rows,
-    fields_hbm, evap_hbm, coal_hbm, fold_hbm, owner_hbm, cell_hbm, pid_hbm,
-    obuf, recv_buf, side_in,
+    fields_hbm, evap_hbm, coal_hbm, fold_hbm, width_hbm, owner_hbm, cell_hbm, pid_hbm,
+    obuf, recv_buf, side_in, widths,
     fbuf, tbuf, edge_in, upright_buf, fold, cols_out, cols_near, cols_in, par, send_buf,
-    evap_ref, coal_ref, owner_ref, cell_ref, pid_ref, picks, in_slot,
+    evap_ref, coal_ref, width_ref, owner_ref, cell_ref, pid_ref, picks, in_slot,
     in_sem, arg_sem, halo_send, halo_recv, row_send, row_recv, side_out, side_send, side_recv,
 ):
     owners = n_slab * n_plane
@@ -95,7 +95,7 @@
     spray_args = [
         pltpu.make_async_copy(source, target, arg_sem.at[k])
         for k, (source, target) in enumerate(
-            ((evap_hbm, evap_ref), (coal_hbm, coal_ref), (fold_hbm, fold))
+            ((evap_hbm, evap_ref), (coal_hbm, coal_ref), (fold_hbm, fold), (width_hbm, width_ref))
         )
     ]
 
@@ -362,19 +362,16 @@
                     src_ref=side_out,
                     dst_ref=side_in.at[me],
                     send_sem=side_send.at[row * n_plane + j],
-                    recv_sem=side_recv.at[me],
+                    recv_sem=side_recv,
                     device_id=(1, row, j),
                     device_id_type=MESH,
                 ).start()
-
-        for i in range(n_slab):
-            row = jnp.where(2 * s < n_slab, n_slab - 1 - i, i)
             for j in range(n_plane):
                 pltpu.make_async_remote_copy(
                     src_ref=send_buf.at[row * n_plane + j],
                     dst_ref=recv_buf.at[me],
                     send_sem=row_send.at[row * n_plane + j],
-                    recv_sem=row_recv.at[me],
+                    recv_sem=row_recv,
                     device_id=(1, row, j),
                     device_id_type=MESH,
                 ).start()
@@ -422,7 +419,7 @@
                 src_ref=send_buf.at[o],
                 dst_ref=recv_buf.at[me],
                 send_sem=row_send.at[o],
-                recv_sem=row_recv.at[me],
+                recv_sem=row_recv,
                 device_id=(1, o // n_plane, o % n_plane),
                 device_id_type=MESH,
             ).wait_send()
@@ -431,7 +428,7 @@
                 src_ref=side_out,
                 dst_ref=side_in.at[me],
                 send_sem=side_send.at[o],
-                recv_sem=side_recv.at[me],
+                recv_sem=side_recv,
                 device_id=(1, o // n_plane, o % n_plane),
                 device_id_type=MESH,
             ).wait_send()
@@ -449,6 +446,8 @@
         for k in range(sections):
             evap = jnp.where(col_row == k, evap_ref[k], evap)
         speeds = 0.2 + 0.5 * col_row.astype(F32) / (sections - 1)
+        for k in range(width_ref.shape[0]):
+            widths[k] = jnp.full((8, LANES), width_ref[k], F32)
         for a in (0, ca + 1):
             tbuf[a] = jnp.zeros((sections, cb), F32)
 
@@ -522,34 +521,27 @@
         for x, a in enumerate((0, ca - 1)):
             scatter_row(a, mixed[:, x * cb : (x + 1) * cb])
 
-        @pl.loop(0, owners)
-        def _(o):
+        for whole, sent, got in (
+            (recv_buf, row_send, row_recv),
+            (side_in, side_send, side_recv),
+        ):
             pltpu.make_async_remote_copy(
-                src_ref=send_buf.at[o],
-                dst_ref=recv_buf.at[o],
-                send_sem=row_send.at[o],
-                recv_sem=row_recv.at[o],
+                src_ref=whole,
+                dst_ref=whole,
+                send_sem=sent.at[0],
+                recv_sem=got,
                 device_id=(0, s, p),
                 device_id_type=MESH,
             ).wait_recv()
 
-            pltpu.make_async_remote_copy(
-                src_ref=side_out,
-                dst_ref=side_in.at[o],
-                send_sem=side_send.at[o],
-                recv_sem=side_recv.at[o],
-                device_id=(0, s, p),
-                device_id_type=MESH,
-            ).wait_recv()
-
 
 def finish(
     n_plane, owners, sections, ca, cb,
-    held, rows_in, sides_in, width_hbm,
+    held, rows_in, sides_in, widths,
     out_hbm,
-    obuf, flat, par, mass, left_even, left_odd, right_even, right_odd, width_ref, arg_sem, out_sem,
+    obuf, flat, par, mass, left_even, left_odd, right_even, right_odd, out_sem,
 ):
-    plumes = width_ref.shape[0]
+    plumes = widths.shape[0]
     rows = sections * ca
     g = lax.axis_index("group")
     whole = held.reshape(sections, 2 * ca + PAD, LANES).at[:, pl.ds(0, 2 * ca), :]
@@ -563,10 +555,6 @@
 
     @pl.when(g == 1)
     def _():
-        fetch = pltpu.make_async_copy(width_hbm, width_ref, arg_sem)
-        fetch.start()
-        fill = pltpu.make_async_copy(whole, obuf, out_sem.at[PIECES])
-        fill.start()
         half_cb = cb // 2
         pad = n_plane * LINES
         flat[pl.ds(0, pad)] = jnp.zeros((pad, LANES), F32)
@@ -580,7 +568,6 @@
                 for x in range(3):
                     flat[pl.ds(at + 16 + x, 1)] = sides_in[b * 8 + o, x]
 
-        fetch.wait()
         sub = lax.broadcasted_iota(jnp.int32, (8, LANES), 0)
 
         @pl.loop(0, owners // 8, unroll=2)
@@ -624,9 +611,9 @@
                 ):
                     flux += jnp.where(here, pick(table, 2 * line + base), 0.0)
                     skew += jnp.where(here, pick(table, 2 * line + base + ca), 0.0)
-                spread = jnp.full((8, LANES), width_ref[0], F32)
+                spread = widths[0]
                 for k in range(1, plumes):
-                    spread = jnp.where(got[3] == float(k), width_ref[k], spread)
+                    spread = jnp.where(got[3] == float(k), widths[k], spread)
                 values = (
                     jnp.where(place != 0, jnp.sqrt(1.0 + flux * flux), 0.0),
                     (sections - 1) * jax.nn.sigmoid(skew),
@@ -659,7 +646,7 @@
                     jnp.broadcast_to(mass[k : k + 1], (ca, span)).astype(BF16) * mask
                 )
 
-        def add(left, right, first, count):
+        def add(left, right, first, count, base):
             added = dot_last(left[first * ca : (first + count) * ca], right[...])
             tiles = jnp.stack(
                 [
@@ -668,25 +655,27 @@
                 ],
                 axis=1,
             )
-            obuf[first : first + count] += tiles.reshape(count, 2 * ca, LANES)
+            obuf[first : first + count] = base[first : first + count] + tiles.reshape(
+                count, 2 * ca, LANES
+            )
 
         build(0, left_even, right_even)
-        fill.wait()
         steps = owners // SOURCES
 
-        @pl.loop(0, steps // 2 - 1)
+        add(left_even, right_even, 0, sections, whole)
+        build(1, left_odd, right_odd)
+
+        @pl.loop(1, steps // 2)
         def _(i):
-            add(left_even, right_even, 0, sections)
+            add(left_odd, right_odd, 0, sections, obuf)
+            build(2 * i, left_even, right_even)
+            add(left_even, right_even, 0, sections, obuf)
             build(2 * i + 1, left_odd, right_odd)
-            add(left_odd, right_odd, 0, sections)
-            build(2 * i + 2, left_even, right_even)
-
-        add(left_even, right_even, 0, sections)
-        build(steps - 1, left_odd, right_odd)
+
         each = sections // PIECES
         stores = []
         for c in range(PIECES):
-            add(left_odd, right_odd, c * each, each)
+            add(left_odd, right_odd, c * each, each, obuf)
             at = pl.ds(c * each, each)
             stores.append(
                 pltpu.make_async_copy(obuf.at[at], out_whole.at[at], out_sem.at[c])
@@ -705,15 +694,16 @@
     kept = fold.shape[1]
     hbm = pl.BlockSpec(memory_space=pl.ANY)
     vmem = pl.BlockSpec(memory_space=pltpu.VMEM)
-    held, rows_in, sides_in = pl.pallas_call(
+    held, rows_in, sides_in, widths = pl.pallas_call(
         functools.partial(kernel, n_slab, n_plane, sections, ca, cb, exit_rows),
         out_shape=[
             pltpu.VMEM((2 * rows + sections * PAD, LANES), F32),
             pltpu.VMEM((owners, 16, LANES), BF16),
             pltpu.VMEM((owners, 3, 1, LANES), F32),
+            pltpu.VMEM(plume_width.shape + (8, LANES), F32),
         ],
-        in_specs=[hbm] * 7,
-        out_specs=[vmem] * 3,
+        in_specs=[hbm] * 8,
+        out_specs=[vmem] * 4,
         scratch_shapes=[
             pltpu.VMEM((2 * rows + sections * PAD, LANES), F32),
             pltpu.VMEM((ca + 2, sections, cb), F32),
@@ -727,6 +717,7 @@
             pltpu.VMEM((owners, 16, LANES), BF16),
             pltpu.SMEM(evap_rates.shape, F32),
             pltpu.VMEM(coal_kernel.shape, BF16),
+            pltpu.SMEM(plume_width.shape, F32),
             pltpu.VMEM((1, exit_rows), jnp.int32),
             pltpu.VMEM((1, exit_rows), jnp.int32),
             pltpu.VMEM((1, exit_rows), jnp.int32),
@@ -737,23 +728,23 @@
             pltpu.SemaphoreType.DMA((4,)),
             pltpu.SemaphoreType.DMA((4,)),
             pltpu.SemaphoreType.DMA((owners,)),
-            pltpu.SemaphoreType.DMA((owners,)),
+            pltpu.SemaphoreType.DMA,
             pltpu.VMEM((3, 1, LANES), F32),
             pltpu.SemaphoreType.DMA((owners,)),
-            pltpu.SemaphoreType.DMA((owners,)),
+            pltpu.SemaphoreType.DMA,
         ],
         compiler_params=pltpu.CompilerParams(
             collective_id=0, has_side_effects=True, vmem_limit_bytes=VMEM_BYTES
         ),
     )(
-        fields.reshape(rows // 8, 8, 2, LANES).transpose(0, 2, 1, 3).reshape(2 * rows, LANES), evap_rates, coal_kernel, fold,
+        fields.reshape(rows // 8, 8, 2, LANES).transpose(0, 2, 1, 3).reshape(2 * rows, LANES), evap_rates, coal_kernel, fold, plume_width,
         owner_map, deposit_cell, plume_ids,
     )
     span = SOURCES * SLOTS
     out = pl.pallas_call(
         functools.partial(finish, n_plane, owners, sections, ca, cb),
         out_shape=jax.ShapeDtypeStruct((2 * rows, LANES), F32),
-        in_specs=[vmem, vmem, vmem, hbm],
+        in_specs=[vmem] * 4,
         out_specs=hbm,
         scratch_shapes=[
             pltpu.VMEM((sections, 2 * ca, LANES), F32),
@@ -764,16 +755,14 @@
             pltpu.VMEM((rows, span), BF16),
             pltpu.VMEM((cb, span), BF16),
             pltpu.VMEM((cb, span), BF16),
-            pltpu.SMEM(plume_width.shape, F32),
-            pltpu.SemaphoreType.DMA,
-            pltpu.SemaphoreType.DMA((PIECES + 1,)),
+            pltpu.SemaphoreType.DMA((PIECES,)),
         ],
         compiler_params=pltpu.CompilerParams(vmem_limit_bytes=VMEM_BYTES),
     )(
         pltpu.with_memory_space_constraint(held, pltpu.VMEM),
         pltpu.with_memory_space_constraint(rows_in, pltpu.VMEM),
         pltpu.with_memory_space_constraint(sides_in, pltpu.VMEM),
-        plume_width,
+        pltpu.with_memory_space_constraint(widths, pltpu.VMEM),
     )
     out = out.reshape(rows // 8, 2, 8, LANES).transpose(0, 2, 1, 3)
     return out.reshape(1, sections, ca, cb)

time: 14.5 us -> 13.3 us (0.917)
  Pallas kernels: 14.3 us -> 13.2 us
    pallas_call x1, Pallas kernels: 4.37 us -> 3.61 us  [body(): pl.pallas_call(functools.partial(finish, n_plane, owners, sections, ca, c...]
    pallas_call x1, Pallas kernels: 9.93 us -> 9.58 us  [body(): pl.pallas_call(functools.partial(kernel, n_slab, n_plane, sections, ca, c...]
where the time goes in v6:
time: 13.3 us; the launch traced here: 13.2 us
  Pallas kernels  13.2 us (99%)
    pallas_call x1, Pallas kernels, body(): pl.pallas_call(functools.partial(kernel, n_slab, n_plane, sections, ca, c...  9.58 us
    pallas_call x1, Pallas kernels, body(): pl.pallas_call(functools.partial(finish, n_plane, owners, sections, ca, c...  3.61 us

profile of v6, /device:TPU:5, one launch (start us, length us, event | category | flops | bytes accessed | tf_op | source)
XLA Modules:
  0.0 13.2 jit_solution(5524486728426198148)
XLA Ops:
  0.0 9.6 %shard_map.82 = (f32[2304,128]{1,0:T(8,128)S(1)}, bf16[16,16,128]{2,1,0:T(8,128)(2,1)S(1)}, f32[16,3,1,128]{3,2,1,0:T(1,128)S(1)}, f32[8,8,128]{2,1,0:T(8,128)S(1)}) custom-call(f32[2048,128]{1,0:T(8,128)} %bitcast.10, f32[32]{0:T(128)} %evap_hbm.1, bf16[32,1024]{1,0:T(8,128)(2,1)} %coal_hbm.1, bf16[1024,640]{1,0:T(8,128)(2,1)} %constant.2.clone.fold_hbm, ...), custom_call_target="tpu_custom_call" | custom-call | tf_op jit(solution)/shard_map/pallas_call | solution.py:697
  9.6 3.6 %shard_map.83 = f32[2048,128]{1,0:T(8,128)} custom-call(f32[2304,128]{1,0:T(8,128)S(1)} %get-tuple-element.9.held, bf16[16,16,128]{2,1,0:T(8,128)(2,1)S(1)} %get-tuple-element.10.rows_in, f32[16,3,1,128]{3,2,1,0:T(1,128)S(1)} %get-tuple-element.11.sides_in, f32[8,8,128]{2,1,0:T(8,128)S(1)} %get-tuple-element.12.widths), custom_call_target="tpu_custom_call" | custom-call | tf_op jit(solution)/shard_map/pallas_call | solution.py:744

commit v7 on v6

--- a/solution.py
+++ b/solution.py
@@ -17,7 +17,7 @@
 PAD = 8
 LINES = 24
 SOURCES = 4
-PIECES = 2
+PIECES = (3, 1)
 VMEM_BYTES = 56 * 1024 * 1024
 
 cfl_nozzle = 0.35
@@ -60,7 +60,7 @@
     n_slab, n_plane, sections, ca, cb, exit_rows,
     fields_hbm, evap_hbm, coal_hbm, fold_hbm, width_hbm, owner_hbm, cell_hbm, pid_hbm,
     obuf, recv_buf, side_in, widths,
-    fbuf, tbuf, edge_in, upright_buf, fold, cols_out, cols_near, cols_in, par, send_buf,
+    fbuf, tbuf, edge_out, edge_in, upright_buf, fold, cols_out, cols_near, cols_in, par, send_buf,
     evap_ref, coal_ref, width_ref, owner_ref, cell_ref, pid_ref, picks, in_slot,
     in_sem, arg_sem, halo_send, halo_recv, row_send, row_recv, side_out, side_send, side_recv,
 ):
@@ -136,8 +136,8 @@
 
     def halo(kind, target):
         source, landing = (
-            (tbuf.at[ca], edge_in.at[0]),
-            (tbuf.at[1], edge_in.at[1]),
+            (edge_out.at[1], edge_in.at[0]),
+            (edge_out.at[0], edge_in.at[1]),
             (cols_out.at[1], cols_in.at[0]),
             (cols_out.at[0], cols_in.at[1]),
         )[kind]
@@ -159,8 +159,10 @@
                 halo(kind, outgoing[kind][1]).start()
 
     def extract_columns():
-        for a in (0, ca - 1):
-            tbuf[a + 1] = gather_row(fbuf, a)
+        for x, a in enumerate((0, ca - 1)):
+            edge = gather_row(fbuf, a)
+            tbuf[a + 1] = edge
+            edge_out[x] = edge.astype(BF16)
 
         lane = lax.broadcasted_iota(jnp.int32, (8, LANES), 1)
         line = lax.broadcasted_iota(jnp.int32, (8, LANES), 0)
@@ -183,7 +185,7 @@
 
             @pl.when(jnp.logical_not(sides[kind][0]))
             def _():
-                landing[...] = jnp.zeros(landing.shape, F32)
+                landing[...] = jnp.zeros(landing.shape, landing.dtype)
 
     def wait_halo():
         for kind in range(4):
@@ -356,7 +358,7 @@
         pl.semaphore_wait(barrier, near + owners)
 
         for i in range(n_slab):
-            row = jnp.where(2 * s < n_slab, n_slab - 1 - i, i)
+            row = i
             for j in range(n_plane):
                 pltpu.make_async_remote_copy(
                     src_ref=side_out,
@@ -410,8 +412,9 @@
             axis=1,
         ).reshape(sections, 2 * ca, LANES)
         for side, a in enumerate((0, ca - 1)):
+            edge = diffusion * edge_in[side].astype(F32)
             for h in range(2):
-                obuf[lines(a, h), :] += diffusion * edge_in[side, :, h * LANES : (h + 1) * LANES]
+                obuf[lines(a, h), :] += edge[:, h * LANES : (h + 1) * LANES]
 
         @pl.loop(0, owners)
         def _(o):
@@ -481,7 +484,7 @@
 
         wait_halo()
         for side, a in enumerate((0, ca + 1)):
-            tbuf[a] = edge_in[side]
+            tbuf[a] = edge_in[side].astype(F32)
         tile_lane = lax.broadcasted_iota(jnp.int32, (8, LANES), 1)
         wide_lane = lax.broadcasted_iota(jnp.int32, (sections, LANES), 1)
 
@@ -646,8 +649,11 @@
                     jnp.broadcast_to(mass[k : k + 1], (ca, span)).astype(BF16) * mask
                 )
 
-        def add(left, right, first, count, base):
-            added = dot_last(left[first * ca : (first + count) * ca], right[...])
+        def add(pairs, first, count, base):
+            added = sum(
+                dot_last(left[first * ca : (first + count) * ca], right[...])
+                for left, right in pairs
+            )
             tiles = jnp.stack(
                 [
                     added[:, h * LANES : (h + 1) * LANES].reshape(count * ca // 8, 8, LANES)
@@ -659,24 +665,30 @@
                 count, 2 * ca, LANES
             )
 
-        build(0, left_even, right_even)
+        even = left_even, right_even
+        odd = left_odd, right_odd
         steps = owners // SOURCES
-
-        add(left_even, right_even, 0, sections, whole)
-        build(1, left_odd, right_odd)
-
-        @pl.loop(1, steps // 2)
+        build(0, *even)
+        add([even], 0, sections, whole)
+        build(1, *odd)
+
+        @pl.loop(1, steps // 2 - 1)
         def _(i):
-            add(left_odd, right_odd, 0, sections, obuf)
-            build(2 * i, left_even, right_even)
-            add(left_even, right_even, 0, sections, obuf)
-            build(2 * i + 1, left_odd, right_odd)
-
-        each = sections // PIECES
+            add([odd], 0, sections, obuf)
+            build(2 * i, *even)
+            add([even], 0, sections, obuf)
+            build(2 * i + 1, *odd)
+
+        add([odd], 0, sections, obuf)
+        build(steps - 2, *even)
+        build(steps - 1, *odd)
         stores = []
-        for c in range(PIECES):
-            add(left_odd, right_odd, c * each, each, obuf)
-            at = pl.ds(c * each, each)
+        first = 0
+        for c, part in enumerate(PIECES):
+            count = part * sections // sum(PIECES)
+            add([even, odd], first, count, obuf)
+            at = pl.ds(first, count)
+            first += count
             stores.append(
                 pltpu.make_async_copy(obuf.at[at], out_whole.at[at], out_sem.at[c])
             )
@@ -707,7 +719,8 @@
         scratch_shapes=[
             pltpu.VMEM((2 * rows + sections * PAD, LANES), F32),
             pltpu.VMEM((ca + 2, sections, cb), F32),
-            pltpu.VMEM((2, sections, cb), F32),
+            pltpu.VMEM((2, sections, cb), BF16),
+            pltpu.VMEM((2, sections, cb), BF16),
             pltpu.VMEM((3, sections, LANES), F32),
             pltpu.VMEM((sections * sections, kept), BF16),
             pltpu.VMEM((2, rows // LANES, LANES), F32),
@@ -755,7 +768,7 @@
             pltpu.VMEM((rows, span), BF16),
             pltpu.VMEM((cb, span), BF16),
             pltpu.VMEM((cb, span), BF16),
-            pltpu.SemaphoreType.DMA((PIECES,)),
+            pltpu.SemaphoreType.DMA((len(PIECES),)),
         ],
         compiler_params=pltpu.CompilerParams(vmem_limit_bytes=VMEM_BYTES),
     )(

time: 13.3 us -> 13.3 us (level)
  no operation moved by 1% of the time
where the time goes in v7:
time: 13.3 us; the launch traced here: 13.2 us
  Pallas kernels  13.2 us (99%)
    pallas_call x1, Pallas kernels, body(): pl.pallas_call(functools.partial(kernel, n_slab, n_plane, sections, ca, c...  9.58 us
    pallas_call x1, Pallas kernels, body(): pl.pallas_call(functools.partial(finish, n_plane, owners, sections, ca, c...  3.59 us

profile of v7, /device:TPU:5, one launch (start us, length us, event | category | flops | bytes accessed | tf_op | source)
XLA Modules:
  0.0 13.2 jit_solution(2232996170557368975)
XLA Ops:
  0.0 9.6 %shard_map.82 = (f32[2304,128]{1,0:T(8,128)S(1)}, bf16[16,16,128]{2,1,0:T(8,128)(2,1)S(1)}, f32[16,3,1,128]{3,2,1,0:T(1,128)S(1)}, f32[8,8,128]{2,1,0:T(8,128)S(1)}) custom-call(f32[2048,128]{1,0:T(8,128)} %bitcast.10, f32[32]{0:T(128)} %evap_hbm.1, bf16[32,1024]{1,0:T(8,128)(2,1)} %coal_hbm.1, bf16[1024,640]{1,0:T(8,128)(2,1)} %constant.2.clone.fold_hbm, ...), custom_call_target="tpu_custom_call" | custom-call | tf_op jit(solution)/shard_map/pallas_call | solution.py:709
  9.6 3.6 %shard_map.83 = f32[2048,128]{1,0:T(8,128)} custom-call(f32[2304,128]{1,0:T(8,128)S(1)} %get-tuple-element.9.held, bf16[16,16,128]{2,1,0:T(8,128)(2,1)S(1)} %get-tuple-element.10.rows_in, f32[16,3,1,128]{3,2,1,0:T(1,128)S(1)} %get-tuple-element.11.sides_in, f32[8,8,128]{2,1,0:T(8,128)S(1)} %get-tuple-element.12.widths), custom_call_target="tpu_custom_call" | custom-call | tf_op jit(solution)/shard_map/pallas_call | solution.py:757
